TPU v7x, 128 devices: a whole 4x4x4 slice. The times are simulated.
128 devices in a mesh: vocab: 16 (over y, z), feat: 8 (over x, core).
Axes of the slice: x: 4, y: 4, z: 4, core: 2. Of those that a mesh axis runs over, the one named last changes fastest.
Arguments:
- hidden: bfloat16 [2048, 4096], P('feat'), may hold values from -64 to 64
- out_head: bfloat16 [131072, 4096], P(('vocab', 'feat')), may hold values from -0.28125 to 0.28125
- out_proj: bfloat16 [131072, 128], P(('vocab', 'feat')), may hold values from -5 to 5
- in_proj: bfloat16 [4096, 128], replicated, may hold values from -0.09375 to 0.09375
- targets: int32 [2048], replicated, may hold values from 0 to 131071
- seq_ids: int32 [2048], replicated, may hold values from 0 to 15, never falling along the last dimension, each value on 1 to 256 neighbouring positions
- grad_store: bfloat16 [32768, 16384], P('vocab', 'feat'), may hold values from -0.01953125 to 0.01953125
Outputs:
- influence: float32 [32768, 16], P(('vocab', 'feat'))
All inputs are finite; a program needn't handle non-finite values.
Results may differ from a plain program's by a relative error of at most 0.003.
Values may be sent and summed in bfloat16 or wider, within the bound.
No kernel may reach another device: no remote copies, remote signals or barrier semaphores. Data moves between devices by JAX's collectives and lax.ppermute only.
A program may use at most 128 MiB of HBM per device.

v0:
```python
import functools

import jax
import jax.numpy as jnp
from jax import lax
from jax.experimental import pallas as pl
from jax.experimental.pallas import tpu as pltpu
from jax.sharding import Mesh
from jax.sharding import PartitionSpec as P

SEQS = 16
ALL = ("y", "z", "x", "c")
TILE = 256
LIMIT = 26 * 1024 * 1024
AHEAD = 2
BF = jnp.bfloat16
F32 = jnp.float32


def index(y, z, x, c):
    return (((y % 4) * 4 + z % 4) * 4 + x % 4) * 2 + c


def move(value, target):
    pairs = [
        (index(y, z, x, c), index(*target(y, z, x, c)))
        for y in range(4)
        for z in range(4)
        for x in range(4)
        for c in range(2)
    ]
    return lax.ppermute(value, ALL, pairs)


def along_x(y, z, x, c):
    return (y, z, x + 1 - 2 * c, c)


def along_x_crossed(y, z, x, c):
    return (y, z, x - 1 + 2 * c, 1 - c)


def along_y(y, z, x, c):
    return (y + 1 - 2 * c, z, x, c)


def along_z(y, z, x, c):
    return (y, z + 1 - 2 * c, x, c)


def to_sibling(y, z, x, c):
    return (y, z, x, 1 - c)


def rows_kernel(plan, count, *refs):
    sources, results, sems = refs[:count], refs[count:-1], refs[-1]
    copies = [
        pltpu.make_async_copy(
            sources[source].at[start : start + rows, :],
            results[to].at[at : at + rows, :],
            sems.at[n],
        )
        for n, (source, start, rows, to, at) in enumerate(plan)
    ]
    for copy in copies:
        copy.start()
    for copy in copies:
        copy.wait()


def rows_of(plan, sources, lengths):
    away = pl.BlockSpec(memory_space=pl.ANY)
    width = sources[0].shape[1]
    return pl.pallas_call(
        functools.partial(rows_kernel, plan, len(sources)),
        in_specs=[away] * len(sources),
        out_specs=[away] * len(lengths),
        out_shape=[jax.ShapeDtypeStruct((n, width), BF) for n in lengths],
        scratch_shapes=[pltpu.SemaphoreType.DMA((len(plan),))],
        compiler_params=pltpu.CompilerParams(vmem_limit_bytes=16 * 1024 * 1024),
        cost_estimate=pl.CostEstimate(
            flops=0, bytes_accessed=4 * width * sum(lengths), transcendentals=0
        ),
    )(*sources)


def flash_kernel(sizes, stream, *refs):
    count = len(sizes)
    pieces, heads = refs[:count], refs[count : count + 2]
    projs, in_ref = refs[count + 2 : count + 4], refs[count + 4]
    out_ref, lse_ref, side_ref = refs[count + 5 : count + 8]
    tok, held, scores, sems, head_sem = refs[count + 8 : count + 13]
    rows = heads[0].shape[0]

    copies = []
    at = 0
    for number, (size, piece) in enumerate(zip(sizes, pieces)):
        copies.append(pltpu.make_async_copy(piece, tok.at[at : at + size, :], sems.at[number]))
        at += size
    blocks = []
    bounds = (0, 256, 512, 1024, 1536, 2048) if stream else (1024, 1536, 2048)
    for low, high in zip(bounds, bounds[1:]):
        head, shift = heads[low // rows], low // rows * rows
        at = low if stream else low - rows
        blocks.append(
            pltpu.make_async_copy(
                head.at[low - shift : high - shift, :],
                held.at[at : at + high - low, :],
                head_sem.at[len(blocks)],
            )
        )
    others = []
    if stream:
        far = (*projs, in_ref)
        *projs, in_ref = refs[count + 13 : count + 16]
        for n, (source, target) in enumerate(zip(far, (*projs, in_ref))):
            others.append(pltpu.make_async_copy(source, target, refs[count + 16].at[n]))
    for copy in copies + blocks[:AHEAD] + others:
        copy.start()
    for copy in copies:
        copy.wait()

    dims = (((1,), (1,)), ((), ()))
    tile = 1024 if tok.shape[0] <= 256 else 512
    if not stream:
        for low in range(0, rows, tile):
            scores[:, low : low + tile] = lax.dot_general(
                tok[...], heads[0][low : low + tile, :], dims, preferred_element_type=F32
            )
        for block in blocks:
            block.wait()
        for low in range(0, rows, tile):
            scores[:, rows + low : rows + low + tile] = lax.dot_general(
                tok[...], held[low : low + tile, :], dims, preferred_element_type=F32
            )
    else:
        for n, block in enumerate(blocks):
            block.wait()
            if n + AHEAD < len(blocks):
                blocks[n + AHEAD].start()
            low, high = bounds[n], bounds[n + 1]
            scores[:, low:high] = lax.dot_general(
                tok[...], held[low:high, :], dims, preferred_element_type=F32
            )
    for copy in others:
        copy.wait()
    side_ref[...] = jnp.dot(tok[...], in_ref[...], preferred_element_type=F32)

    step = 512
    best = scores[:, 0:step]
    for low in range(step, 2 * rows, step):
        best = jnp.maximum(best, scores[:, low : low + step])
    best = jnp.max(best, axis=1, keepdims=True)
    total = None
    mixed = None
    for low in range(0, 2 * rows, step):
        power = jnp.exp(scores[:, low : low + step] - best)
        total = power if low == 0 else total + power
        proj = projs[low // rows][low % rows : low % rows + step, :]
        part = jnp.dot(power.astype(BF), proj, preferred_element_type=F32)
        mixed = part if low == 0 else mixed + part
    total = jnp.sum(total, axis=1, keepdims=True)
    out_ref[...] = mixed / total
    lse_ref[...] = jnp.broadcast_to(best + jnp.log(total), lse_ref.shape)


def flash(pieces, own, sib, proj_own, proj_sib, in_proj, limit=None):
    sizes = tuple(p.shape[0] for p in pieces)
    n = sum(sizes)
    stream = limit is not None
    rows, depth = own.shape
    rank = proj_own.shape[1]
    here = pl.BlockSpec(memory_space=pltpu.VMEM)
    away = pl.BlockSpec(memory_space=pl.ANY)
    extra = []
    if stream:
        extra = [pltpu.VMEM(a.shape, BF) for a in (proj_own, proj_sib, in_proj)]
        extra.append(pltpu.SemaphoreType.DMA((3,)))
    return pl.pallas_call(
        functools.partial(flash_kernel, sizes, stream),
        in_specs=[away] * len(pieces) + ([away] * 5 if stream else [here, away, here, here, here]),
        out_specs=[here] * 3,
        out_shape=[jax.ShapeDtypeStruct((n, rank), F32)] * 3,
        scratch_shapes=[
            pltpu.VMEM((n, depth), BF),
            pltpu.VMEM((2 * rows if stream else rows, depth), BF),
            pltpu.VMEM((n, 2 * rows), F32),
            pltpu.SemaphoreType.DMA((len(pieces),)),
            pltpu.SemaphoreType.DMA((5 if stream else 2,)),
        ]
        + extra,
        compiler_params=pltpu.CompilerParams(vmem_limit_bytes=(limit << 20) if stream else LIMIT),
        cost_estimate=pl.CostEstimate(
            flops=2 * n * 2 * rows * depth, bytes_accessed=n * depth * 2, transcendentals=0
        ),
    )(*pieces, own, sib, proj_own, proj_sib, in_proj)


def hot_kernel(where, targets_ref, own_ref, sib_ref, out_ref):
    local = out_ref.shape[1]
    total = jnp.zeros(out_ref.shape, F32)
    for which, proj_ref in enumerate((own_ref, sib_ref)):
        for first in range(0, proj_ref.shape[0], TILE):
            ids = where[which] + first + lax.broadcasted_iota(jnp.int32, (TILE, local), 0)
            hot = jnp.where(ids == targets_ref[...], 1.0, 0.0).astype(BF)
            total += lax.dot_general(
                proj_ref[first : first + TILE, :],
                hot,
                (((0,), (0,)), ((), ())),
                preferred_element_type=F32,
            )
    out_ref[...] = total


def hot_rows(where, targets, proj_own, proj_sib):
    here = pl.BlockSpec(memory_space=pltpu.VMEM)
    return pl.pallas_call(
        hot_kernel,
        in_specs=[pl.BlockSpec(memory_space=pltpu.SMEM), here, here, here],
        out_specs=here,
        out_shape=jax.ShapeDtypeStruct((proj_own.shape[1], targets.shape[1]), F32),
        compiler_params=pltpu.CompilerParams(vmem_limit_bytes=16 * 1024 * 1024),
        cost_estimate=pl.CostEstimate(
            flops=2 * 128 * 2048 * 1024, bytes_accessed=1 << 20, transcendentals=0
        ),
    )(where, targets, proj_own, proj_sib)


def pack_kernel(place, *refs):
    outs, lses, sides = refs[0:3], refs[3:6], refs[6:9]
    hot_ref, send_ref, side_ref, out_nat, lse_nat = refs[9:]
    k = place[0]
    spot = [place[1], place[2], place[3], place[4]]

    def put(slot, quarter, source, start, rows, into=0):
        for h in range(rows // 32):
            group = quarter * 2 + into + h
            at = slice(start + 32 * h, start + 32 * h + 32)
            out_nat[group, spot[slot]] = outs[source][at, :]
            lse_nat[group, spot[slot]] = lses[source][at, :]
            side_ref[group, spot[slot]] = sides[source][at, :]

    ky, kz, kd = k ^ 2, k ^ 1, k ^ 3
    for q in range(4):
        put(0, q, 0, 64 * q, 64)
    for n, (slot, quarter) in enumerate(
        [(1, k), (2, k), (1, ky), (2, ky), (1, kz), (2, kz), (3, k), (1, kd)]
    ):
        put(slot, quarter, 1, 64 * n, 64)
    put(3, ky, 2, 0, 64)
    put(2, kd, 2, 64, 32)
    put(3, kz, 2, 96, 64)
    put(2, kd, 2, 160, 32, into=1)
    put(3, kd, 2, 192, 64)

    for group in range(8):
        mixed = jnp.transpose(out_nat[group].reshape(128, 128)).reshape(16, 8, 128)
        lse = jnp.transpose(lse_nat[group].reshape(128, 128))[0:8, :]
        high = lse.astype(BF).astype(F32)
        rest = lse - high
        middle = rest.astype(BF).astype(F32)
        low = rest - middle
        line = lax.broadcasted_iota(jnp.int32, (8, 128), 0)
        stats = jnp.where(
            line == 0, high, jnp.where(line == 1, middle, jnp.where(line == 2, low, 0.0))
        )
        hot = hot_ref[:, group * 128 : group * 128 + 128].reshape(16, 8, 128)
        for part in range(16):
            to = (2 * group + part % 2) * 8 + part // 2
            send_ref[to] = jnp.concatenate([mixed[part], hot[part], stats], axis=0).astype(BF)


def pack(place, results, hot):
    outs, lses, sides = zip(*results)
    return pl.pallas_call(
        pack_kernel,
        in_specs=[pl.BlockSpec(memory_space=pltpu.SMEM)]
        + [pl.BlockSpec(memory_space=pltpu.VMEM)] * 10,
        out_specs=[pl.BlockSpec(memory_space=pltpu.VMEM)] * 2,
        out_shape=[
            jax.ShapeDtypeStruct((128, 24, 128), BF),
            jax.ShapeDtypeStruct((8, 4, 32, 128), F32),
        ],
        scratch_shapes=[pltpu.VMEM((8, 4, 32, 128), F32)] * 2,
        compiler_params=pltpu.CompilerParams(vmem_limit_bytes=16 * 1024 * 1024),
    )(place, *outs, *lses, *sides, hot)


def merge_kernel(got_ref, out_ref):
    lse = (
        got_ref[:, 16:24, :].astype(F32)
    )
    lse = lse[:, 0:1, :] + lse[:, 1:2, :] + lse[:, 2:3, :]
    source = lax.broadcasted_iota(jnp.int32, (128, 1, 128), 0)
    lane = lax.broadcasted_iota(jnp.int32, (128, 1, 128), 2)
    x = lax.div(lax.rem(source, 8), 2)
    c = lax.rem(source, 2)
    other = lax.div(lane, 32) == lax.rem(x + 1, 4)
    kind = jnp.where(other, 1 - c, c)
    halves = []
    for which in range(2):
        mine = kind == which
        best = jnp.max(jnp.where(mine, lse, -3.0e38), axis=0, keepdims=True)
        weight = jnp.where(mine, jnp.exp(jnp.minimum(lse - best, 0.0)), 0.0)
        total = jnp.sum(weight, axis=0)
        mixed = jnp.sum(weight * got_ref[:, 0:8, :].astype(F32), axis=0)
        hot = jnp.sum(jnp.where(mine, got_ref[:, 8:16, :].astype(F32), 0.0), axis=0)
        halves.append(mixed / total - hot)
    both = jnp.concatenate(halves, axis=1)
    for copy in range(16):
        out_ref[copy] = both


def merge(got):
    return pl.pallas_call(
        merge_kernel,
        in_specs=[pl.BlockSpec(memory_space=pltpu.VMEM)],
        out_specs=pl.BlockSpec(memory_space=pltpu.VMEM),
        out_shape=jax.ShapeDtypeStruct((16, 8, 256), F32),
        compiler_params=pltpu.CompilerParams(vmem_limit_bytes=16 * 1024 * 1024),
    )(got)


def score_kernel(
    flags, out_ref, own_hbm, sib_hbm, seq_ref, store_ref, result_ref, own_ref, sib_ref, store, sems, side_sem
):
    rows = store.shape[0] // 8
    copies = [
        pltpu.make_async_copy(
            store_ref.at[n * rows : (n + 1) * rows, :],
            store.at[n * rows : (n + 1) * rows, :],
            sems.at[n],
        )
        for n in range(8)
    ]
    sides = [
        pltpu.make_async_copy(own_hbm, own_ref, side_sem.at[0]),
        pltpu.make_async_copy(sib_hbm, sib_ref, side_sem.at[1]),
    ]
    for copy in sides + copies[:3]:
        copy.start()
    for copy in sides:
        copy.wait()
    total = jnp.zeros((256, 128), F32)
    for group in range(8):
        out = jnp.concatenate([out_ref[2 * group], out_ref[2 * group + 1]], axis=0)
        ids = seq_ref[group : group + 1, :]
        member = lax.broadcasted_iota(jnp.int32, (16, 256), 0) == ids
        spread = jnp.where(member[None, :, :], out[:, None, :], 0.0).reshape(256, 256)
        first, second = [], []
        for spot in range(4):
            own, sib = own_ref[group, spot], sib_ref[group, spot]
            keep = flags[spot] == 0
            first.append(jnp.where(keep, own, sib))
            second.append(jnp.where(keep, sib, own))
        side = jnp.concatenate(first + second, axis=0)
        spread_high = spread.astype(BF)
        spread_low = (spread - spread_high.astype(F32)).astype(BF)
        side_high = side.astype(BF)
        side_low = (side - side_high.astype(F32)).astype(BF)
        for a, b in (
            (spread_high, side_high),
            (spread_high, side_low),
            (spread_low, side_high),
        ):
            total += jnp.dot(a, b, preferred_element_type=F32)
    grads = jnp.concatenate(
        [total[i * 16 : (i + 1) * 16, :].astype(BF) for i in range(16)], axis=1
    )
    for n, copy in enumerate(copies):
        copy.wait()
        if n + 3 < 8:
            copies[n + 3].start()
        result_ref[n] = lax.dot_general(
            grads,
            store[n * rows : (n + 1) * rows, :],
            (((1,), (1,)), ((), ())),
            preferred_element_type=F32,
        )


def score(flags, out, own, sib, seq, store):
    here = pl.BlockSpec(memory_space=pltpu.VMEM)
    away = pl.BlockSpec(memory_space=pl.ANY)
    return pl.pallas_call(
        score_kernel,
        in_specs=[
            pl.BlockSpec(memory_space=pltpu.SMEM),
            here,
            away,
            away,
            here,
            away,
        ],
        out_specs=here,
        out_shape=jax.ShapeDtypeStruct((8, SEQS, store.shape[0] // 8), F32),
        scratch_shapes=[
            pltpu.VMEM(own.shape, F32),
            pltpu.VMEM(own.shape, F32),
            pltpu.VMEM(store.shape, BF),
            pltpu.SemaphoreType.DMA((8,)),
            pltpu.SemaphoreType.DMA((2,)),
        ],
        compiler_params=pltpu.CompilerParams(vmem_limit_bytes=48 * 1024 * 1024),
    )(flags, out, own, sib, seq, store)


def by_place(per_token):
    table = per_token.reshape(4, 2, 256)
    return jnp.stack([table[:, 0], jnp.roll(table[:, 1], 2, axis=0)])


def on_device(hidden, out_head, out_proj, in_proj, targets, seq_ids, grad_store):
    y, z, x, c = (lax.axis_index(name) for name in ALL)
    k = 2 * (y % 2) + z % 2
    sign = 1 - 2 * c
    rows = out_head.shape[0]

    mine = lax.dynamic_slice_in_dim(hidden, k * 64, 64, 0)

    near_a = move(mine, along_x)
    near_b = move(mine, along_x_crossed)
    head_sib = move(out_head, to_sibling)
    proj_sib = move(out_proj, to_sibling)

    first_row = lax.axis_index(ALL) * rows
    sib_row = (lax.axis_index(ALL) + sign) * rows
    places = jnp.arange(4, dtype=jnp.int32)
    kinds = jnp.where(places == (x + 1) % 4, 1 - c, c)
    target_table = by_place(targets)
    local_targets = jnp.where(kinds[:, None] == 0, target_table[0], target_table[1])
    local_targets = local_targets.reshape(4, 8, 32).transpose(1, 0, 2).reshape(1, 1024)
    seq_table = by_place(seq_ids).reshape(2, 4, 8, 32).transpose(2, 0, 1, 3).reshape(8, 256)

    again, local_targets = lax.optimization_barrier((hidden, local_targets))
    mine_d = lax.dynamic_slice_in_dim(again, (3 - k) * 64, 64, 0)

    mine_d, near_a = lax.optimization_barrier((mine_d, near_a))
    near, ahead = rows_of(
        ((0, 0, 64, 0, 0), (1, 0, 64, 0, 64), (0, 0, 64, 1, 0), (2, 0, 64, 1, 64)),
        [near_a, near_b, mine_d],
        [128, 128],
    )
    near_y = move(near, along_y)
    near_z = move(near, along_z)
    ahead = move(ahead, along_x)
    rest = (out_head, head_sib, out_proj, proj_sib, in_proj)
    first = flash([hidden], *rest)
    first, ahead, near_y, near_z = lax.optimization_barrier((first, ahead, near_y, near_z))
    first, local_targets = lax.optimization_barrier((first, local_targets))
    hot = hot_rows(jnp.stack([first_row, sib_row]), local_targets, out_proj, proj_sib)
    last_y, last_z, far_d = rows_of(
        (
            (0, 0, 64, 0, 0),
            (2, 64, 32, 0, 64),
            (0, 0, 64, 1, 0),
            (1, 96, 32, 1, 64),
            (0, 64, 64, 2, 0),
        ),
        [ahead, near_y, near_z],
        [96, 96, 64],
    )
    last_y = move(last_y, along_y)
    last_z = move(last_z, along_z)
    far_d = move(far_d, along_x)
    second = flash([near, near_y, near_z, ahead], *rest)
    third = flash([last_y, last_z, far_d], *rest)
    place = jnp.stack(
        [
            k,
            (x + 2 * c) % 4,
            (x - sign + 2 * c + 4) % 4,
            (x - sign + 2 * (1 - c) + 4) % 4,
            (x + 2 + 2 * c) % 4,
        ]
    ).astype(jnp.int32)
    send, side = pack(place, (first, second, third), hot)
    side_sib = move(side, to_sibling)

    got = lax.all_to_all(send, ALL, 0, 0, tiled=True)

    out = lax.all_to_all(merge(got), ("y", "z"), 0, 0, tiled=True)
    partial = score(kinds.astype(jnp.int32), out, side, side_sib, seq_table, grad_store)
    return jnp.sum(lax.all_to_all(partial, ("x", "c"), 0, 0, tiled=True), axis=0).T


def solution(mesh):
    split = Mesh(mesh.devices.reshape(4, 4, 4, 2), ALL)
    everywhere = P(ALL, None)
    return jax.shard_map(
        on_device,
        mesh=split,
        in_specs=(
            P(("x", "c"), None),
            everywhere,
            everywhere,
            P(),
            P(),
            P(),
            P(("y", "z"), ("x", "c")),
        ),
        out_specs=everywhere,
        check_vma=False,
    )
```

profile of v0, /device:TPU:1, one launch (start us, length us, event | category | flops | bytes accessed | tf_op | source)
XLA Modules:
  0.0 123.7 jit_solution(15625469018112941396)
XLA Ops:
  0.0 1.4 %collective-permute-start = (bf16[1024,4096]{1,0:T(8,128)(2,1)}, bf16[1024,4096]{1,0:T(8,128)(2,1)}, u32[]{:S(2)}, u32[]{:S(2)}) collective-permute-start(bf16[1024,4096]{1,0:T(8,128)(2,1)} %refs_3_.3), channel_id=1, source_target_pairs={{0,1},{1,0},{2,3},{3,2},{4,5},{5,4},{6,7},{7,6},{8,9},{9,8},{10,11... | collective-permute-start | bytes 25165832 | tf_op jit(solution)/shard_map/ppermute | solution.py:32
  2.5 2.6 %collective-permute-start.2 = (bf16[64,4096]{1,0:T(8,128)(2,1)S(1)}, bf16[64,4096]{1,0:T(8,128)(2,1)S(1)}, u32[]{:S(2)}, u32[]{:S(2)}) collective-permute-start(bf16[64,4096]{1,0:T(8,128)(2,1)S(1)} %constant_dynamic-slice_fusion), channel_id=1, source_target_pairs={{0,2},{1,7},{2,4},{3,1},{4,6},{5,3},{6,0},{7,5},{8,10},{9,15},{10,... | collective-permute-start | bytes 1572872 | tf_op jit(solution)/shard_map/ppermute | solution.py:32
  7.5 8.2 %collective-permute-done.2.refs_0_ = bf16[64,4096]{1,0:T(8,128)(2,1)S(1)} collective-permute-done((bf16[64,4096]{1,0:T(8,128)(2,1)S(1)}, bf16[64,4096]{1,0:T(8,128)(2,1)S(1)}, u32[]{:S(2)}, u32[]{:S(2)}) %collective-permute-start.2) | collective-permute-done | bytes 524320 | tf_op jit(solution)/shard_map/ppermute | solution.py:32
  16.5 1.4 %shard_map.74 = (bf16[128,4096]{1,0:T(8,128)(2,1)}, bf16[128,4096]{1,0:T(8,128)(2,1)}) custom-call(bf16[64,4096]{1,0:T(8,128)(2,1)S(1)} %collective-permute-done.2.refs_0_, bf16[64,4096]{1,0:T(8,128)(2,1)S(1)} %collective-permute-done.3.refs_1_, bf16[64,4096]{1,0:T(8,128)(2,1)S(1)} %constant_dynamic-slice_fusion.1.refs_2_), custom_call_target="tpu_custom_call" | custom-call | bytes 4194304 | tf_op jit(solution)/shard_map/pallas_call | solution.py:74
  17.9 3.5 %collective-permute-start.4 = (bf16[128,4096]{1,0:T(8,128)(2,1)}, bf16[128,4096]{1,0:T(8,128)(2,1)S(1)}, u32[]{:S(2)}, u32[]{:S(2)}) collective-permute-start(bf16[128,4096]{1,0:T(8,128)(2,1)} %get-tuple-element.41), channel_id=1, source_target_pairs={{0,2},{1,7},{2,4},{3,1},{4,6},{5,3},{6,0},{7,5},{8,10},{9,15},{10,... | collective-permute-start | bytes 3145736 | tf_op jit(solution)/shard_map/ppermute | solution.py:32
  21.5 2.7 %collective-permute-start.5 = (bf16[128,4096]{1,0:T(8,128)(2,1)}, bf16[128,4096]{1,0:T(8,128)(2,1)S(1)}, u32[]{:S(2)}, u32[]{:S(2)}) collective-permute-start(bf16[128,4096]{1,0:T(8,128)(2,1)} %get-tuple-element.42.refs_0_), channel_id=1, source_target_pairs={{0,32},{1,97},{2,34},{3,99},{4,36},{5,101},{6,38},{7,103},{8,40},{... | collective-permute-start | bytes 3145736 | tf_op jit(solution)/shard_map/ppermute | solution.py:32
  24.2 3.8 %collective-permute-start.6 = (bf16[128,4096]{1,0:T(8,128)(2,1)}, bf16[128,4096]{1,0:T(8,128)(2,1)S(1)}, u32[]{:S(2)}, u32[]{:S(2)}) collective-permute-start(bf16[128,4096]{1,0:T(8,128)(2,1)} %get-tuple-element.42.refs_0_), channel_id=1, source_target_pairs={{0,8},{1,25},{2,10},{3,27},{4,12},{5,29},{6,14},{7,31},{8,16},{9,1... | collective-permute-start | bytes 3145736 | tf_op jit(solution)/shard_map/ppermute | solution.py:32
  28.1 1.6 %collective-permute-done.1.refs_4_.refs_7_.refs_6_.sib_ref = bf16[1024,128]{1,0:T(8,128)(2,1)S(1)} collective-permute-done((bf16[1024,128]{1,0:T(8,128)(2,1)}, bf16[1024,128]{1,0:T(8,128)(2,1)S(1)}, u32[]{:S(2)}, u32[]{:S(2)}) %collective-permute-start.1) | collective-permute-done | bytes 262176 | tf_op jit(solution)/shard_map/ppermute | solution.py:32
  29.7 3.4 %copy-done = bf16[1024,4096]{1,0:T(8,128)(2,1)S(1)} copy-done((bf16[1024,4096]{1,0:T(8,128)(2,1)S(1)}, bf16[1024,4096]{1,0:T(8,128)(2,1)}, u32[]{:S(2)}) %copy-start) | copy-done | bytes 8388632
  33.1 1.6 %copy-done.2 = bf16[256,4096]{1,0:T(8,128)(2,1)S(1)} copy-done((bf16[256,4096]{1,0:T(8,128)(2,1)S(1)}, bf16[256,4096]{1,0:T(8,128)(2,1)}, u32[]{:S(2)}) %copy-start.2) | copy-done | bytes 2097176
  34.7 1.2 copy-done.3
  36.9 7.2 %shard_map.73 = (f32[256,128]{1,0:T(8,128)S(1)}, f32[256,128]{1,0:T(8,128)S(1)}, f32[256,128]{1,0:T(8,128)S(1)}) custom-call(bf16[256,4096]{1,0:T(8,128)(2,1)S(1)} %copy-done.2, bf16[1024,4096]{1,0:T(8,128)(2,1)S(1)} %copy-done, bf16[1024,4096]{1,0:T(8,128)(2,1)} %collective-permute-done.refs_2_.refs_5_.refs_4_, bf16[1024,128]{1,0:T(8,128)(2,1)S(1)} %copy-done.5, ...), custom_call_target="tpu_custom_call" | custom-call | flops 4294967296 | bytes 2097152 | tf_op jit(solution)/shard_map/pallas_call | solution.py:179
  45.9 1.3 %shard_map.78.refs_9_ = f32[128,1024]{1,0:T(8,128)S(1)} custom-call(s32[2]{0:T(128)S(1)} %pad_add_fusion.where, s32[1,1024]{1,0:T(1,128)S(1)} %reshape.44.targets_ref, bf16[1024,128]{1,0:T(8,128)(2,1)S(1)} %copy-done.5, bf16[1024,128]{1,0:T(8,128)(2,1)S(1)} %collective-permute-done.1.refs_4_.refs_7_.refs_6_.sib_ref), custom_call_target="tpu_custom_call" | custom-call | flops 536870912 | bytes 1048576 | tf_op jit(solution)/shard_map/pallas_call | solution.py:217
  47.2 13.6 %shard_map.75 = (f32[512,128]{1,0:T(8,128)S(1)}, f32[512,128]{1,0:T(8,128)S(1)}, f32[512,128]{1,0:T(8,128)S(1)}) custom-call(bf16[128,4096]{1,0:T(8,128)(2,1)} %get-tuple-element.42.refs_0_, bf16[128,4096]{1,0:T(8,128)(2,1)S(1)} %collective-permute-done.5.refs_1_, bf16[128,4096]{1,0:T(8,128)(2,1)S(1)} %collective-permute-done.6.refs_2_, ...), custom_call_target="tpu_custom_call" | custom-call | flops 8589934592 | bytes 4194304 | tf_op jit(solution)/shard_map/pallas_call | solution.py:179
  60.8 7.3 %shard_map.77 = (f32[256,128]{1,0:T(8,128)S(1)}, f32[256,128]{1,0:T(8,128)S(1)}, f32[256,128]{1,0:T(8,128)S(1)}) custom-call(bf16[96,4096]{1,0:T(8,128)(2,1)S(1)} %collective-permute-done.7.refs_0_, bf16[96,4096]{1,0:T(8,128)(2,1)S(1)} %collective-permute-done.8.refs_1_, bf16[64,4096]{1,0:T(8,128)(2,1)S(1)} %collective-permute-done.9.refs_2_, ...), custom_call_target="tpu_custom_call" | custom-call | flops 4294967296 | bytes 2097152 | tf_op jit(solution)/shard_map/pallas_call | solution.py:179
  68.2 1.8 %shard_map.79 = (bf16[128,24,128]{2,1,0:T(8,128)(2,1)}, f32[8,4,32,128]{3,2,1,0:T(8,128)S(1)}) custom-call(s32[5]{0:T(128)S(1)} %stack.38.place, f32[256,128]{1,0:T(8,128)S(1)} %get-tuple-element.47.refs_0_, f32[512,128]{1,0:T(8,128)S(1)} %get-tuple-element.51.refs_1_, f32[256,128]{1,0:T(8,128)S(1)} %get-tuple-element.55.refs_2_, ...), custom_call_target="tpu_custom_call" | custom-call | tf_op jit(solution)/shard_map/pallas_call | solution.py:275
  70.0 8.1 %all-to-all-start = ((bf16[128,24,128]{2,1,0:T(8,128)(2,1)}), bf16[128,24,128]{2,1,0:T(8,128)(2,1)S(1)}, u32[]{:S(2)}, u32[]{:S(2)}) async-start(bf16[128,24,128]{2,1,0:T(8,128)(2,1)} %get-tuple-element.63), calls=%async_computation | async-start | bytes 1572864 | tf_op jit(solution)/shard_map/all_to_all | solution.py:480
  78.1 1.1 collective-permute-start.10
  79.3 15.3 %all-to-all-done.got_ref = bf16[128,24,128]{2,1,0:T(8,128)(2,1)S(1)} async-done(((bf16[128,24,128]{2,1,0:T(8,128)(2,1)}), bf16[128,24,128]{2,1,0:T(8,128)(2,1)S(1)}, u32[]{:S(2)}, u32[]{:S(2)}) %all-to-all-start) | async-done | bytes 786464 | tf_op jit(solution)/shard_map/all_to_all | solution.py:480
  94.6 1.4 %shard_map.80 = f32[16,8,256]{2,1,0:T(8,128)} custom-call(bf16[128,24,128]{2,1,0:T(8,128)(2,1)S(1)} %all-to-all-done.got_ref), custom_call_target="tpu_custom_call" | custom-call | tf_op jit(solution)/shard_map/pallas_call | solution.py:315
  96.0 3.5 %all-to-all-start.1 = ((f32[16,8,256]{2,1,0:T(8,128)}), f32[16,8,256]{2,1,0:T(8,128)S(1)}, u32[]{:S(2)}, u32[]{:S(2)}) async-start(f32[16,8,256]{2,1,0:T(8,128)} %shard_map.80), calls=%async_computation.1 | async-start | bytes 262144 | tf_op jit(solution)/shard_map/all_to_all | solution.py:482
  99.9 6.4 %all-to-all-done.1.out_ref = f32[16,8,256]{2,1,0:T(8,128)S(1)} async-done(((f32[16,8,256]{2,1,0:T(8,128)}), f32[16,8,256]{2,1,0:T(8,128)S(1)}, u32[]{:S(2)}, u32[]{:S(2)}) %all-to-all-start.1) | async-done | bytes 131104 | tf_op jit(solution)/shard_map/all_to_all | solution.py:482
  106.4 7.2 %shard_map.81 = f32[8,16,256]{2,1,0:T(8,128)S(1)} custom-call(s32[4]{0:T(128)S(1)} %get-tuple-element.70.flags, f32[16,8,256]{2,1,0:T(8,128)S(1)} %all-to-all-done.1.out_ref, f32[8,4,32,128]{3,2,1,0:T(8,128)S(1)} %get-tuple-element.64.own_hbm, f32[8,4,32,128]{3,2,1,0:T(8,128)S(1)} %collective-permute-done.10.sib_hbm, s32[8,256]{1,0:T(8,128)S(1)} %reshape.46.seq_ref, ...), custom_call_target="tpu_custom_call" | custom-call | tf_op jit(solution)/shard_map/pallas_call | solution.py:385
  113.6 9.5 %all_to_all.15 = f32[8,16,256]{2,1,0:T(8,128)S(1)} all-to-all(f32[8,16,256]{2,1,0:T(8,128)S(1)} %shard_map.81), channel_id=1, replica_groups=mesh['y'=4,'z'=4,'x'=4,'c'=2] {'x','c'}, dimensions={0} | all-to-all | bytes 262144 | tf_op jit(solution)/shard_map/all_to_all | solution.py:484
  (52 shorter events, 8.1 us)
Async XLA Ops:
  0.0 29.7 %collective-permute-start = (bf16[1024,4096]{1,0:T(8,128)(2,1)}, bf16[1024,4096]{1,0:T(8,128)(2,1)}, u32[]{:S(2)}, u32[]{:S(2)}) collective-permute-start(bf16[1024,4096]{1,0:T(8,128)(2,1)} %refs_3_.3), channel_id=1, source_target_pairs={{0,1},{1,0},{2,3},{3,2},{4,5},{5,4},{6,7},{7,6},{8,9},{9,8},{10,11... | collective-permute-start | bytes 25165832 | tf_op jit(solution)/shard_map/ppermute | solution.py:32
  2.5 13.2 %collective-permute-start.2 = (bf16[64,4096]{1,0:T(8,128)(2,1)S(1)}, bf16[64,4096]{1,0:T(8,128)(2,1)S(1)}, u32[]{:S(2)}, u32[]{:S(2)}) collective-permute-start(bf16[64,4096]{1,0:T(8,128)(2,1)S(1)} %constant_dynamic-slice_fusion), channel_id=1, source_target_pairs={{0,2},{1,7},{2,4},{3,1},{4,6},{5,3},{6,0},{7,5},{8,10},{9,15},{10,... | collective-permute-start | bytes 1572872 | tf_op jit(solution)/shard_map/ppermute | solution.py:32
  5.1 11.4 %collective-permute-start.3 = (bf16[64,4096]{1,0:T(8,128)(2,1)S(1)}, bf16[64,4096]{1,0:T(8,128)(2,1)S(1)}, u32[]{:S(2)}, u32[]{:S(2)}) collective-permute-start(bf16[64,4096]{1,0:T(8,128)(2,1)S(1)} %constant_dynamic-slice_fusion), channel_id=1, source_target_pairs={{0,7},{1,2},{2,1},{3,4},{4,3},{5,6},{6,5},{7,0},{8,15},{9,10},{10,... | collective-permute-start | bytes 1572872 | tf_op jit(solution)/shard_map/ppermute | solution.py:32
  17.9 26.2 %collective-permute-start.4 = (bf16[128,4096]{1,0:T(8,128)(2,1)}, bf16[128,4096]{1,0:T(8,128)(2,1)S(1)}, u32[]{:S(2)}, u32[]{:S(2)}) collective-permute-start(bf16[128,4096]{1,0:T(8,128)(2,1)} %get-tuple-element.41), channel_id=1, source_target_pairs={{0,2},{1,7},{2,4},{3,1},{4,6},{5,3},{6,0},{7,5},{8,10},{9,15},{10,... | collective-permute-start | bytes 3145736 | tf_op jit(solution)/shard_map/ppermute | solution.py:32
  21.5 22.6 %collective-permute-start.5 = (bf16[128,4096]{1,0:T(8,128)(2,1)}, bf16[128,4096]{1,0:T(8,128)(2,1)S(1)}, u32[]{:S(2)}, u32[]{:S(2)}) collective-permute-start(bf16[128,4096]{1,0:T(8,128)(2,1)} %get-tuple-element.42.refs_0_), channel_id=1, source_target_pairs={{0,32},{1,97},{2,34},{3,99},{4,36},{5,101},{6,38},{7,103},{8,40},{... | collective-permute-start | bytes 3145736 | tf_op jit(solution)/shard_map/ppermute | solution.py:32
  24.2 19.9 %collective-permute-start.6 = (bf16[128,4096]{1,0:T(8,128)(2,1)}, bf16[128,4096]{1,0:T(8,128)(2,1)S(1)}, u32[]{:S(2)}, u32[]{:S(2)}) collective-permute-start(bf16[128,4096]{1,0:T(8,128)(2,1)} %get-tuple-element.42.refs_0_), channel_id=1, source_target_pairs={{0,8},{1,25},{2,10},{3,27},{4,12},{5,29},{6,14},{7,31},{8,16},{9,1... | collective-permute-start | bytes 3145736 | tf_op jit(solution)/shard_map/ppermute | solution.py:32
  28.0 1.7 %collective-permute-start.1 = (bf16[1024,128]{1,0:T(8,128)(2,1)}, bf16[1024,128]{1,0:T(8,128)(2,1)S(1)}, u32[]{:S(2)}, u32[]{:S(2)}) collective-permute-start(bf16[1024,128]{1,0:T(8,128)(2,1)} %own_ref.1), channel_id=1, source_target_pairs={{0,1},{1,0},{2,3},{3,2},{4,5},{5,4},{6,7},{7,6},{8,9},{9,8},{10,11... | collective-permute-start | bytes 786440 | tf_op jit(solution)/shard_map/ppermute | solution.py:32
  29.7 3.4 %copy-start = (bf16[1024,4096]{1,0:T(8,128)(2,1)S(1)}, bf16[1024,4096]{1,0:T(8,128)(2,1)}, u32[]{:S(2)}) copy-start(bf16[1024,4096]{1,0:T(8,128)(2,1)} %refs_3_.3) | copy-start | bytes 25165828
  33.1 1.6 %copy-start.2 = (bf16[256,4096]{1,0:T(8,128)(2,1)S(1)}, bf16[256,4096]{1,0:T(8,128)(2,1)}, u32[]{:S(2)}) copy-start(bf16[256,4096]{1,0:T(8,128)(2,1)} %refs_0_.1) | copy-start | bytes 6291460
  34.7 1.2 copy-start.3
  35.9 0.9 copy-start.5
  36.9 10.3 %copy-start.1 = (bf16[1024,4096]{1,0:T(8,128)(2,1)S(1)}, bf16[1024,4096]{1,0:T(8,128)(2,1)}, u32[]{:S(2)}) copy-start(bf16[1024,4096]{1,0:T(8,128)(2,1)} %refs_3_.3) | copy-start | bytes 25165828
  36.9 10.3 %copy-start.4 = (bf16[4096,128]{1,0:T(8,128)(2,1)S(1)}, bf16[4096,128]{1,0:T(8,128)(2,1)}, u32[]{:S(2)}) copy-start(bf16[4096,128]{1,0:T(8,128)(2,1)} %refs_7_.1) | copy-start | bytes 3145732
  36.9 10.3 %copy-start.6 = (bf16[1024,128]{1,0:T(8,128)(2,1)S(1)}, bf16[1024,128]{1,0:T(8,128)(2,1)}, u32[]{:S(2)}) copy-start(bf16[1024,128]{1,0:T(8,128)(2,1)} %own_ref.1) | copy-start | bytes 786436
  44.3 16.5 %collective-permute-start.7 = (bf16[96,4096]{1,0:T(8,128)(2,1)S(1)}, bf16[96,4096]{1,0:T(8,128)(2,1)S(1)}, u32[]{:S(2)}, u32[]{:S(2)}) collective-permute-start(bf16[96,4096]{1,0:T(8,128)(2,1)S(1)} %get-tuple-element.52), channel_id=1, source_target_pairs={{0,32},{1,97},{2,34},{3,99},{4,36},{5,101},{6,38},{7,103},{8,40},{... | collective-permute-start | bytes 2359304 | tf_op jit(solution)/shard_map/ppermute | solution.py:32
  44.9 16.0 %collective-permute-start.8 = (bf16[96,4096]{1,0:T(8,128)(2,1)S(1)}, bf16[96,4096]{1,0:T(8,128)(2,1)S(1)}, u32[]{:S(2)}, u32[]{:S(2)}) collective-permute-start(bf16[96,4096]{1,0:T(8,128)(2,1)S(1)} %get-tuple-element.53), channel_id=1, source_target_pairs={{0,8},{1,25},{2,10},{3,27},{4,12},{5,29},{6,14},{7,31},{8,16},{9,1... | collective-permute-start | bytes 2359304 | tf_op jit(solution)/shard_map/ppermute | solution.py:32
  45.0 15.8 %collective-permute-start.9 = (bf16[64,4096]{1,0:T(8,128)(2,1)S(1)}, bf16[64,4096]{1,0:T(8,128)(2,1)S(1)}, u32[]{:S(2)}, u32[]{:S(2)}) collective-permute-start(bf16[64,4096]{1,0:T(8,128)(2,1)S(1)} %get-tuple-element.54), channel_id=1, source_target_pairs={{0,2},{1,7},{2,4},{3,1},{4,6},{5,3},{6,0},{7,5},{8,10},{9,15},{10,... | collective-permute-start | bytes 1572872 | tf_op jit(solution)/shard_map/ppermute | solution.py:32
  60.8 18.4 %copy-start.7 = (s32[2048]{0:T(1024)S(1)}, s32[2048]{0:T(1024)}, u32[]{:S(2)}) copy-start(s32[2048]{0:T(1024)} %param.12) | copy-start | bytes 24580
  70.0 24.6 %all-to-all-start = ((bf16[128,24,128]{2,1,0:T(8,128)(2,1)}), bf16[128,24,128]{2,1,0:T(8,128)(2,1)S(1)}, u32[]{:S(2)}, u32[]{:S(2)}) async-start(bf16[128,24,128]{2,1,0:T(8,128)(2,1)} %get-tuple-element.63), calls=%async_computation | async-start | bytes 1572864 | tf_op jit(solution)/shard_map/all_to_all | solution.py:480
  78.1 21.8 %collective-permute-start.10 = (f32[8,4,32,128]{3,2,1,0:T(8,128)S(1)}, f32[8,4,32,128]{3,2,1,0:T(8,128)S(1)}, u32[]{:S(2)}, u32[]{:S(2)}) collective-permute-start(f32[8,4,32,128]{3,2,1,0:T(8,128)S(1)} %get-tuple-element.64.own_hbm), channel_id=1, source_target_pairs={{0,1},{1,0},{2,3},{3,2},{4,5},{5,4},{6,7},{7,6},{8,9},{9,8},{10,11... | collective-permute-start | bytes 1572872 | tf_op jit(solution)/shard_map/ppermute | solution.py:32
  96.0 10.3 %all-to-all-start.1 = ((f32[16,8,256]{2,1,0:T(8,128)}), f32[16,8,256]{2,1,0:T(8,128)S(1)}, u32[]{:S(2)}, u32[]{:S(2)}) async-start(f32[16,8,256]{2,1,0:T(8,128)} %shard_map.80), calls=%async_computation.1 | async-start | bytes 262144 | tf_op jit(solution)/shard_map/all_to_all | solution.py:482
where the time goes:
time: 124 us
  Pallas kernels  41.4 us (33%)
  waiting for transfers between devices  32.4 us (26%)
  starting transfers between devices  28.5 us (23%)
  local copies, waits for them, and re-layouts  10.9 us (9%)
  blocking collectives  9.5 us (8%)
    pallas_call x3, Pallas kernels, flash(): pl.pallas_call(functools.partial(flash_kernel, sizes, stream), in_specs=[...  28.1 us
    ppermute x11, starting transfers between devices, move(): return lax.ppermute(value, ALL, pairs)  16.9 us
    all_to_all x1, waiting for transfers between devices, on_device(): got = lax.all_to_all(send, ALL, 0, 0, tiled=True)  15.3 us
    ppermute x11, waiting for transfers between devices, move(): return lax.ppermute(value, ALL, pairs)  10.6 us
    all_to_all x1, blocking collectives, on_device(): lax.all_to_all(partial, ('x', 'c'), 0, 0, tiled=True)  9.5 us
    all_to_all x1, starting transfers between devices, on_device(): got = lax.all_to_all(send, ALL, 0, 0, tiled=True)  8.1 us
    pallas_call x1, Pallas kernels, score(): pl.pallas_call(score_kernel, in_specs=[pl.BlockSpec(memory_space=pltpu.SM...  7.19 us
    unnamed x16, local copies, waits for them, and re-layouts  7.16 us
  transfers between devices with their start and end apart: 13, of which 5 were waited for; matrix products, arithmetic and copies ran while one was open for 3% of the time, Pallas kernels for 20%

commit v1 on v0

--- a/solution.py
+++ b/solution.py
@@ -435,7 +435,7 @@
     again, local_targets = lax.optimization_barrier((hidden, local_targets))
     mine_d = lax.dynamic_slice_in_dim(again, (3 - k) * 64, 64, 0)
 
-    mine_d, near_a = lax.optimization_barrier((mine_d, near_a))
+    mine_d, near_a, proj_sib = lax.optimization_barrier((mine_d, near_a, proj_sib))
     near, ahead = rows_of(
         ((0, 0, 64, 0, 0), (1, 0, 64, 0, 64), (0, 0, 64, 1, 0), (2, 0, 64, 1, 64)),
         [near_a, near_b, mine_d],

time: 124 us -> 120 us (0.968)
  waiting for transfers between devices: 32.4 us -> 30 us
  starting transfers between devices: 28.5 us -> 27.1 us
    ppermute x11, waiting for transfers between devices: 10.6 us -> 8.2 us  [move(): return lax.ppermute(value, ALL, pairs)]
    all_to_all x1, starting transfers between devices: 8.1 us -> 6.33 us  [on_device(): got = lax.all_to_all(send, ALL, 0, 0, tiled=True)]
  transfers between devices with their start and end apart: 13 -> 13, of which waited for: 5 -> 5; matrix products, arithmetic and copies ran while one was open for 3% -> 3% of each run, Pallas kernels for 20% -> 21%
where the time goes in v1:
time: 120 us
  Pallas kernels  41.4 us (34%)
  waiting for transfers between devices  30 us (25%)
  starting transfers between devices  27.1 us (23%)
  local copies, waits for them, and re-layouts  10.9 us (9%)
  blocking collectives  9.5 us (8%)
    pallas_call x3, Pallas kernels, flash(): pl.pallas_call(functools.partial(flash_kernel, sizes, stream), in_specs=[...  28.1 us
    ppermute x11, starting transfers between devices, move(): return lax.ppermute(value, ALL, pairs)  17.3 us
    all_to_all x1, waiting for transfers between devices, on_device(): got = lax.all_to_all(send, ALL, 0, 0, tiled=True)  15.3 us
    all_to_all x1, blocking collectives, on_device(): lax.all_to_all(partial, ('x', 'c'), 0, 0, tiled=True)  9.5 us
    ppermute x11, waiting for transfers between devices, move(): return lax.ppermute(value, ALL, pairs)  8.2 us
    pallas_call x1, Pallas kernels, score(): pl.pallas_call(score_kernel, in_specs=[pl.BlockSpec(memory_space=pltpu.SM...  7.19 us
    unnamed x16, local copies, waits for them, and re-layouts  7.16 us
    all_to_all x1, waiting for transfers between devices, on_device(): out = lax.all_to_all(merge(got), ('y', 'z'), 0, 0, tiled=True)  6.43 us
  transfers between devices with their start and end apart: 13, of which 5 were waited for; matrix products, arithmetic and copies ran while one was open for 3% of the time, Pallas kernels for 21%

profile of v1, /device:TPU:1, one launch (start us, length us, event | category | flops | bytes accessed | tf_op | source)
XLA Modules:
  0.0 119.9 jit_solution(16466770440211653409)
XLA Ops:
  0.0 1.4 %collective-permute-start = (bf16[1024,4096]{1,0:T(8,128)(2,1)}, bf16[1024,4096]{1,0:T(8,128)(2,1)}, u32[]{:S(2)}, u32[]{:S(2)}) collective-permute-start(bf16[1024,4096]{1,0:T(8,128)(2,1)} %refs_3_.3), channel_id=1, source_target_pairs={{0,1},{1,0},{2,3},{3,2},{4,5},{5,4},{6,7},{7,6},{8,9},{9,8},{10,11... | collective-permute-start | bytes 25165832 | tf_op jit(solution)/shard_map/ppermute | solution.py:32
  2.5 2.6 %collective-permute-start.1 = (bf16[64,4096]{1,0:T(8,128)(2,1)S(1)}, bf16[64,4096]{1,0:T(8,128)(2,1)S(1)}, u32[]{:S(2)}, u32[]{:S(2)}) collective-permute-start(bf16[64,4096]{1,0:T(8,128)(2,1)S(1)} %constant_dynamic-slice_fusion), channel_id=1, source_target_pairs={{0,2},{1,7},{2,4},{3,1},{4,6},{5,3},{6,0},{7,5},{8,10},{9,15},{10,... | collective-permute-start | bytes 1572872 | tf_op jit(solution)/shard_map/ppermute | solution.py:32
  7.2 1.1 constant_dynamic-slice_fusion.1.refs_2_
  8.3 6.5 %collective-permute-done.2.refs_4_.refs_7_.refs_6_.sib_ref = bf16[1024,128]{1,0:T(8,128)(2,1)S(1)} collective-permute-done((bf16[1024,128]{1,0:T(8,128)(2,1)}, bf16[1024,128]{1,0:T(8,128)(2,1)S(1)}, u32[]{:S(2)}, u32[]{:S(2)}) %collective-permute-start.2) | collective-permute-done | bytes 262176 | tf_op jit(solution)/shard_map/ppermute | solution.py:32
  16.5 1.4 %shard_map.74 = (bf16[128,4096]{1,0:T(8,128)(2,1)}, bf16[128,4096]{1,0:T(8,128)(2,1)}) custom-call(bf16[64,4096]{1,0:T(8,128)(2,1)S(1)} %collective-permute-done.1.refs_0_, bf16[64,4096]{1,0:T(8,128)(2,1)S(1)} %collective-permute-done.3.refs_1_, bf16[64,4096]{1,0:T(8,128)(2,1)S(1)} %constant_dynamic-slice_fusion.1.refs_2_), custom_call_target="tpu_custom_call" | custom-call | bytes 4194304 | tf_op jit(solution)/shard_map/pallas_call | solution.py:74
  17.9 3.5 %collective-permute-start.4 = (bf16[128,4096]{1,0:T(8,128)(2,1)}, bf16[128,4096]{1,0:T(8,128)(2,1)S(1)}, u32[]{:S(2)}, u32[]{:S(2)}) collective-permute-start(bf16[128,4096]{1,0:T(8,128)(2,1)} %get-tuple-element.43), channel_id=1, source_target_pairs={{0,2},{1,7},{2,4},{3,1},{4,6},{5,3},{6,0},{7,5},{8,10},{9,15},{10,... | collective-permute-start | bytes 3145736 | tf_op jit(solution)/shard_map/ppermute | solution.py:32
  21.5 2.7 %collective-permute-start.5 = (bf16[128,4096]{1,0:T(8,128)(2,1)}, bf16[128,4096]{1,0:T(8,128)(2,1)S(1)}, u32[]{:S(2)}, u32[]{:S(2)}) collective-permute-start(bf16[128,4096]{1,0:T(8,128)(2,1)} %get-tuple-element.44.refs_0_), channel_id=1, source_target_pairs={{0,32},{1,97},{2,34},{3,99},{4,36},{5,101},{6,38},{7,103},{8,40},{... | collective-permute-start | bytes 3145736 | tf_op jit(solution)/shard_map/ppermute | solution.py:32
  24.2 3.8 %collective-permute-start.6 = (bf16[128,4096]{1,0:T(8,128)(2,1)}, bf16[128,4096]{1,0:T(8,128)(2,1)S(1)}, u32[]{:S(2)}, u32[]{:S(2)}) collective-permute-start(bf16[128,4096]{1,0:T(8,128)(2,1)} %get-tuple-element.44.refs_0_), channel_id=1, source_target_pairs={{0,8},{1,25},{2,10},{3,27},{4,12},{5,29},{6,14},{7,31},{8,16},{9,1... | collective-permute-start | bytes 3145736 | tf_op jit(solution)/shard_map/ppermute | solution.py:32
  28.1 3.4 %copy-done = bf16[1024,4096]{1,0:T(8,128)(2,1)S(1)} copy-done((bf16[1024,4096]{1,0:T(8,128)(2,1)S(1)}, bf16[1024,4096]{1,0:T(8,128)(2,1)}, u32[]{:S(2)}) %copy-start) | copy-done | bytes 8388632
  31.5 1.6 %copy-done.2 = bf16[256,4096]{1,0:T(8,128)(2,1)S(1)} copy-done((bf16[256,4096]{1,0:T(8,128)(2,1)S(1)}, bf16[256,4096]{1,0:T(8,128)(2,1)}, u32[]{:S(2)}) %copy-start.2) | copy-done | bytes 2097176
  33.1 1.2 %copy-done.3 = bf16[4096,128]{1,0:T(8,128)(2,1)S(1)} copy-done((bf16[4096,128]{1,0:T(8,128)(2,1)S(1)}, bf16[4096,128]{1,0:T(8,128)(2,1)}, u32[]{:S(2)}) %copy-start.3) | copy-done | bytes 1048600
  35.3 7.2 %shard_map.73 = (f32[256,128]{1,0:T(8,128)S(1)}, f32[256,128]{1,0:T(8,128)S(1)}, f32[256,128]{1,0:T(8,128)S(1)}) custom-call(bf16[256,4096]{1,0:T(8,128)(2,1)S(1)} %copy-done.2, bf16[1024,4096]{1,0:T(8,128)(2,1)S(1)} %copy-done, bf16[1024,4096]{1,0:T(8,128)(2,1)} %collective-permute-done.refs_2_.refs_5_.refs_4_, bf16[1024,128]{1,0:T(8,128)(2,1)S(1)} %copy-done.5, ...), custom_call_target="tpu_custom_call" | custom-call | flops 4294967296 | bytes 2097152 | tf_op jit(solution)/shard_map/pallas_call | solution.py:179
  43.9 1.3 %shard_map.78.refs_9_ = f32[128,1024]{1,0:T(8,128)S(1)} custom-call(s32[2]{0:T(128)S(1)} %pad_add_fusion.where, s32[1,1024]{1,0:T(1,128)S(1)} %reshape.44.targets_ref, bf16[1024,128]{1,0:T(8,128)(2,1)S(1)} %copy-done.5, bf16[1024,128]{1,0:T(8,128)(2,1)S(1)} %collective-permute-done.2.refs_4_.refs_7_.refs_6_.sib_ref), custom_call_target="tpu_custom_call" | custom-call | flops 536870912 | bytes 1048576 | tf_op jit(solution)/shard_map/pallas_call | solution.py:217
  45.2 13.6 %shard_map.75 = (f32[512,128]{1,0:T(8,128)S(1)}, f32[512,128]{1,0:T(8,128)S(1)}, f32[512,128]{1,0:T(8,128)S(1)}) custom-call(bf16[128,4096]{1,0:T(8,128)(2,1)} %get-tuple-element.44.refs_0_, bf16[128,4096]{1,0:T(8,128)(2,1)S(1)} %collective-permute-done.5.refs_1_, bf16[128,4096]{1,0:T(8,128)(2,1)S(1)} %collective-permute-done.6.refs_2_, ...), custom_call_target="tpu_custom_call" | custom-call | flops 8589934592 | bytes 4194304 | tf_op jit(solution)/shard_map/pallas_call | solution.py:179
  58.8 7.3 %shard_map.77 = (f32[256,128]{1,0:T(8,128)S(1)}, f32[256,128]{1,0:T(8,128)S(1)}, f32[256,128]{1,0:T(8,128)S(1)}) custom-call(bf16[96,4096]{1,0:T(8,128)(2,1)S(1)} %collective-permute-done.7.refs_0_, bf16[96,4096]{1,0:T(8,128)(2,1)S(1)} %collective-permute-done.8.refs_1_, bf16[64,4096]{1,0:T(8,128)(2,1)S(1)} %collective-permute-done.9.refs_2_, ...), custom_call_target="tpu_custom_call" | custom-call | flops 4294967296 | bytes 2097152 | tf_op jit(solution)/shard_map/pallas_call | solution.py:179
  66.1 1.8 %shard_map.79 = (bf16[128,24,128]{2,1,0:T(8,128)(2,1)}, f32[8,4,32,128]{3,2,1,0:T(8,128)S(1)}) custom-call(s32[5]{0:T(128)S(1)} %stack.38.place, f32[256,128]{1,0:T(8,128)S(1)} %get-tuple-element.49.refs_0_, f32[512,128]{1,0:T(8,128)S(1)} %get-tuple-element.53.refs_1_, f32[256,128]{1,0:T(8,128)S(1)} %get-tuple-element.57.refs_2_, ...), custom_call_target="tpu_custom_call" | custom-call | tf_op jit(solution)/shard_map/pallas_call | solution.py:275
  67.9 6.3 %all-to-all-start = ((bf16[128,24,128]{2,1,0:T(8,128)(2,1)}), bf16[128,24,128]{2,1,0:T(8,128)(2,1)S(1)}, u32[]{:S(2)}, u32[]{:S(2)}) async-start(bf16[128,24,128]{2,1,0:T(8,128)(2,1)} %get-tuple-element.65), calls=%async_computation | async-start | bytes 1572864 | tf_op jit(solution)/shard_map/all_to_all | solution.py:480
  74.3 1.1 collective-permute-start.10
  75.5 15.3 %all-to-all-done.got_ref = bf16[128,24,128]{2,1,0:T(8,128)(2,1)S(1)} async-done(((bf16[128,24,128]{2,1,0:T(8,128)(2,1)}), bf16[128,24,128]{2,1,0:T(8,128)(2,1)S(1)}, u32[]{:S(2)}, u32[]{:S(2)}) %all-to-all-start) | async-done | bytes 786464 | tf_op jit(solution)/shard_map/all_to_all | solution.py:480
  90.8 1.4 %shard_map.80 = f32[16,8,256]{2,1,0:T(8,128)} custom-call(bf16[128,24,128]{2,1,0:T(8,128)(2,1)S(1)} %all-to-all-done.got_ref), custom_call_target="tpu_custom_call" | custom-call | tf_op jit(solution)/shard_map/pallas_call | solution.py:315
  92.2 3.5 %all-to-all-start.1 = ((f32[16,8,256]{2,1,0:T(8,128)}), f32[16,8,256]{2,1,0:T(8,128)S(1)}, u32[]{:S(2)}, u32[]{:S(2)}) async-start(f32[16,8,256]{2,1,0:T(8,128)} %shard_map.80), calls=%async_computation.1 | async-start | bytes 262144 | tf_op jit(solution)/shard_map/all_to_all | solution.py:482
  96.1 6.4 %all-to-all-done.1.out_ref = f32[16,8,256]{2,1,0:T(8,128)S(1)} async-done(((f32[16,8,256]{2,1,0:T(8,128)}), f32[16,8,256]{2,1,0:T(8,128)S(1)}, u32[]{:S(2)}, u32[]{:S(2)}) %all-to-all-start.1) | async-done | bytes 131104 | tf_op jit(solution)/shard_map/all_to_all | solution.py:482
  102.5 7.2 %shard_map.81 = f32[8,16,256]{2,1,0:T(8,128)S(1)} custom-call(s32[4]{0:T(128)S(1)} %get-tuple-element.72.flags, f32[16,8,256]{2,1,0:T(8,128)S(1)} %all-to-all-done.1.out_ref, f32[8,4,32,128]{3,2,1,0:T(8,128)S(1)} %get-tuple-element.66.own_hbm, f32[8,4,32,128]{3,2,1,0:T(8,128)S(1)} %collective-permute-done.10.sib_hbm, s32[8,256]{1,0:T(8,128)S(1)} %reshape.46.seq_ref, ...), custom_call_target="tpu_custom_call" | custom-call | tf_op jit(solution)/shard_map/pallas_call | solution.py:385
  109.7 9.5 %all_to_all.15 = f32[8,16,256]{2,1,0:T(8,128)S(1)} all-to-all(f32[8,16,256]{2,1,0:T(8,128)S(1)} %shard_map.81), channel_id=1, replica_groups=mesh['y'=4,'z'=4,'x'=4,'c'=2] {'x','c'}, dimensions={0} | all-to-all | bytes 262144 | tf_op jit(solution)/shard_map/all_to_all | solution.py:484
  (52 shorter events, 8.4 us)
Async XLA Ops:
  0.0 28.1 %collective-permute-start = (bf16[1024,4096]{1,0:T(8,128)(2,1)}, bf16[1024,4096]{1,0:T(8,128)(2,1)}, u32[]{:S(2)}, u32[]{:S(2)}) collective-permute-start(bf16[1024,4096]{1,0:T(8,128)(2,1)} %refs_3_.3), channel_id=1, source_target_pairs={{0,1},{1,0},{2,3},{3,2},{4,5},{5,4},{6,7},{7,6},{8,9},{9,8},{10,11... | collective-permute-start | bytes 25165832 | tf_op jit(solution)/shard_map/ppermute | solution.py:32
  2.5 13.2 %collective-permute-start.1 = (bf16[64,4096]{1,0:T(8,128)(2,1)S(1)}, bf16[64,4096]{1,0:T(8,128)(2,1)S(1)}, u32[]{:S(2)}, u32[]{:S(2)}) collective-permute-start(bf16[64,4096]{1,0:T(8,128)(2,1)S(1)} %constant_dynamic-slice_fusion), channel_id=1, source_target_pairs={{0,2},{1,7},{2,4},{3,1},{4,6},{5,3},{6,0},{7,5},{8,10},{9,15},{10,... | collective-permute-start | bytes 1572872 | tf_op jit(solution)/shard_map/ppermute | solution.py:32
  5.1 11.4 %collective-permute-start.3 = (bf16[64,4096]{1,0:T(8,128)(2,1)S(1)}, bf16[64,4096]{1,0:T(8,128)(2,1)S(1)}, u32[]{:S(2)}, u32[]{:S(2)}) collective-permute-start(bf16[64,4096]{1,0:T(8,128)(2,1)S(1)} %constant_dynamic-slice_fusion), channel_id=1, source_target_pairs={{0,7},{1,2},{2,1},{3,4},{4,3},{5,6},{6,5},{7,0},{8,15},{9,10},{10,... | collective-permute-start | bytes 1572872 | tf_op jit(solution)/shard_map/ppermute | solution.py:32
  5.2 9.5 %collective-permute-start.2 = (bf16[1024,128]{1,0:T(8,128)(2,1)}, bf16[1024,128]{1,0:T(8,128)(2,1)S(1)}, u32[]{:S(2)}, u32[]{:S(2)}) collective-permute-start(bf16[1024,128]{1,0:T(8,128)(2,1)} %own_ref.1), channel_id=1, source_target_pairs={{0,1},{1,0},{2,3},{3,2},{4,5},{5,4},{6,7},{7,6},{8,9},{9,8},{10,11... | collective-permute-start | bytes 786440 | tf_op jit(solution)/shard_map/ppermute | solution.py:32
  17.9 24.6 %collective-permute-start.4 = (bf16[128,4096]{1,0:T(8,128)(2,1)}, bf16[128,4096]{1,0:T(8,128)(2,1)S(1)}, u32[]{:S(2)}, u32[]{:S(2)}) collective-permute-start(bf16[128,4096]{1,0:T(8,128)(2,1)} %get-tuple-element.43), channel_id=1, source_target_pairs={{0,2},{1,7},{2,4},{3,1},{4,6},{5,3},{6,0},{7,5},{8,10},{9,15},{10,... | collective-permute-start | bytes 3145736 | tf_op jit(solution)/shard_map/ppermute | solution.py:32
  21.5 21.1 %collective-permute-start.5 = (bf16[128,4096]{1,0:T(8,128)(2,1)}, bf16[128,4096]{1,0:T(8,128)(2,1)S(1)}, u32[]{:S(2)}, u32[]{:S(2)}) collective-permute-start(bf16[128,4096]{1,0:T(8,128)(2,1)} %get-tuple-element.44.refs_0_), channel_id=1, source_target_pairs={{0,32},{1,97},{2,34},{3,99},{4,36},{5,101},{6,38},{7,103},{8,40},{... | collective-permute-start | bytes 3145736 | tf_op jit(solution)/shard_map/ppermute | solution.py:32
  24.2 18.3 %collective-permute-start.6 = (bf16[128,4096]{1,0:T(8,128)(2,1)}, bf16[128,4096]{1,0:T(8,128)(2,1)S(1)}, u32[]{:S(2)}, u32[]{:S(2)}) collective-permute-start(bf16[128,4096]{1,0:T(8,128)(2,1)} %get-tuple-element.44.refs_0_), channel_id=1, source_target_pairs={{0,8},{1,25},{2,10},{3,27},{4,12},{5,29},{6,14},{7,31},{8,16},{9,1... | collective-permute-start | bytes 3145736 | tf_op jit(solution)/shard_map/ppermute | solution.py:32
  28.1 3.4 %copy-start = (bf16[1024,4096]{1,0:T(8,128)(2,1)S(1)}, bf16[1024,4096]{1,0:T(8,128)(2,1)}, u32[]{:S(2)}) copy-start(bf16[1024,4096]{1,0:T(8,128)(2,1)} %refs_3_.3) | copy-start | bytes 25165828
  31.5 1.6 %copy-start.2 = (bf16[256,4096]{1,0:T(8,128)(2,1)S(1)}, bf16[256,4096]{1,0:T(8,128)(2,1)}, u32[]{:S(2)}) copy-start(bf16[256,4096]{1,0:T(8,128)(2,1)} %refs_0_.1) | copy-start | bytes 6291460
  33.1 1.2 %copy-start.3 = (bf16[4096,128]{1,0:T(8,128)(2,1)S(1)}, bf16[4096,128]{1,0:T(8,128)(2,1)}, u32[]{:S(2)}) copy-start(bf16[4096,128]{1,0:T(8,128)(2,1)} %refs_7_.1) | copy-start | bytes 3145732
  34.3 0.9 copy-start.5
  35.3 9.9 %copy-start.1 = (bf16[1024,4096]{1,0:T(8,128)(2,1)S(1)}, bf16[1024,4096]{1,0:T(8,128)(2,1)}, u32[]{:S(2)}) copy-start(bf16[1024,4096]{1,0:T(8,128)(2,1)} %refs_3_.3) | copy-start | bytes 25165828
  35.3 9.9 %copy-start.4 = (bf16[4096,128]{1,0:T(8,128)(2,1)S(1)}, bf16[4096,128]{1,0:T(8,128)(2,1)}, u32[]{:S(2)}) copy-start(bf16[4096,128]{1,0:T(8,128)(2,1)} %refs_7_.1) | copy-start | bytes 3145732
  35.3 9.9 %copy-start.6 = (bf16[1024,128]{1,0:T(8,128)(2,1)S(1)}, bf16[1024,128]{1,0:T(8,128)(2,1)}, u32[]{:S(2)}) copy-start(bf16[1024,128]{1,0:T(8,128)(2,1)} %own_ref.1) | copy-start | bytes 786436
  42.8 16.0 %collective-permute-start.7 = (bf16[96,4096]{1,0:T(8,128)(2,1)S(1)}, bf16[96,4096]{1,0:T(8,128)(2,1)S(1)}, u32[]{:S(2)}, u32[]{:S(2)}) collective-permute-start(bf16[96,4096]{1,0:T(8,128)(2,1)S(1)} %get-tuple-element.54), channel_id=1, source_target_pairs={{0,32},{1,97},{2,34},{3,99},{4,36},{5,101},{6,38},{7,103},{8,40},{... | collective-permute-start | bytes 2359304 | tf_op jit(solution)/shard_map/ppermute | solution.py:32
  43.3 15.5 %collective-permute-start.8 = (bf16[96,4096]{1,0:T(8,128)(2,1)S(1)}, bf16[96,4096]{1,0:T(8,128)(2,1)S(1)}, u32[]{:S(2)}, u32[]{:S(2)}) collective-permute-start(bf16[96,4096]{1,0:T(8,128)(2,1)S(1)} %get-tuple-element.55), channel_id=1, source_target_pairs={{0,8},{1,25},{2,10},{3,27},{4,12},{5,29},{6,14},{7,31},{8,16},{9,1... | collective-permute-start | bytes 2359304 | tf_op jit(solution)/shard_map/ppermute | solution.py:32
  43.8 15.0 %collective-permute-start.9 = (bf16[64,4096]{1,0:T(8,128)(2,1)S(1)}, bf16[64,4096]{1,0:T(8,128)(2,1)S(1)}, u32[]{:S(2)}, u32[]{:S(2)}) collective-permute-start(bf16[64,4096]{1,0:T(8,128)(2,1)S(1)} %get-tuple-element.56), channel_id=1, source_target_pairs={{0,2},{1,7},{2,4},{3,1},{4,6},{5,3},{6,0},{7,5},{8,10},{9,15},{10,... | collective-permute-start | bytes 1572872 | tf_op jit(solution)/shard_map/ppermute | solution.py:32
  58.8 16.7 %copy-start.7 = (s32[2048]{0:T(1024)S(1)}, s32[2048]{0:T(1024)}, u32[]{:S(2)}) copy-start(s32[2048]{0:T(1024)} %param.12) | copy-start | bytes 24580
  67.9 22.9 %all-to-all-start = ((bf16[128,24,128]{2,1,0:T(8,128)(2,1)}), bf16[128,24,128]{2,1,0:T(8,128)(2,1)S(1)}, u32[]{:S(2)}, u32[]{:S(2)}) async-start(bf16[128,24,128]{2,1,0:T(8,128)(2,1)} %get-tuple-element.65), calls=%async_computation | async-start | bytes 1572864 | tf_op jit(solution)/shard_map/all_to_all | solution.py:480
  74.3 21.8 %collective-permute-start.10 = (f32[8,4,32,128]{3,2,1,0:T(8,128)S(1)}, f32[8,4,32,128]{3,2,1,0:T(8,128)S(1)}, u32[]{:S(2)}, u32[]{:S(2)}) collective-permute-start(f32[8,4,32,128]{3,2,1,0:T(8,128)S(1)} %get-tuple-element.66.own_hbm), channel_id=1, source_target_pairs={{0,1},{1,0},{2,3},{3,2},{4,5},{5,4},{6,7},{7,6},{8,9},{9,8},{10,11... | collective-permute-start | bytes 1572872 | tf_op jit(solution)/shard_map/ppermute | solution.py:32
  92.2 10.3 %all-to-all-start.1 = ((f32[16,8,256]{2,1,0:T(8,128)}), f32[16,8,256]{2,1,0:T(8,128)S(1)}, u32[]{:S(2)}, u32[]{:S(2)}) async-start(f32[16,8,256]{2,1,0:T(8,128)} %shard_map.80), calls=%async_computation.1 | async-start | bytes 262144 | tf_op jit(solution)/shard_map/all_to_all | solution.py:482

commit v2 on v1

--- a/solution.py
+++ b/solution.py
@@ -68,13 +68,13 @@
         copy.wait()
 
 
-def rows_of(plan, sources, lengths):
+def rows_of(plan, sources, lengths, space=pl.ANY):
     away = pl.BlockSpec(memory_space=pl.ANY)
     width = sources[0].shape[1]
     return pl.pallas_call(
         functools.partial(rows_kernel, plan, len(sources)),
         in_specs=[away] * len(sources),
-        out_specs=[away] * len(lengths),
+        out_specs=[pl.BlockSpec(memory_space=space)] * len(lengths),
         out_shape=[jax.ShapeDtypeStruct((n, width), BF) for n in lengths],
         scratch_shapes=[pltpu.SemaphoreType.DMA((len(plan),))],
         compiler_params=pltpu.CompilerParams(vmem_limit_bytes=16 * 1024 * 1024),
@@ -196,6 +196,69 @@
     )(*pieces, own, sib, proj_own, proj_sib, in_proj)
 
 
+def half_kernel(with_side, tok_far, head_far, proj_far, in_far, *refs):
+    count = 3 if with_side else 2
+    out_ref, lse_ref = refs[:2]
+    tok, held, proj, in_proj, scores, sems = refs[count:]
+    rows = head_far.shape[0]
+    blocks = [
+        pltpu.make_async_copy(
+            head_far.at[low : low + TILE, :], held.at[low : low + TILE, :], sems.at[low // TILE]
+        )
+        for low in range(0, rows, TILE)
+    ]
+    first = pltpu.make_async_copy(tok_far, tok, sems.at[4])
+    others = [pltpu.make_async_copy(proj_far, proj, sems.at[5])]
+    if with_side:
+        others.append(pltpu.make_async_copy(in_far, in_proj, sems.at[6]))
+    for copy in [first] + blocks + others:
+        copy.start()
+    first.wait()
+    for n, block in enumerate(blocks):
+        block.wait()
+        low = n * TILE
+        scores[:, low : low + TILE] = lax.dot_general(
+            tok[...],
+            held[low : low + TILE, :],
+            (((1,), (1,)), ((), ())),
+            preferred_element_type=F32,
+        )
+    for copy in others:
+        copy.wait()
+    if with_side:
+        refs[2][...] = jnp.dot(tok[...], in_proj[...], preferred_element_type=F32)
+    best = jnp.max(scores[...], axis=1, keepdims=True)
+    power = jnp.exp(scores[...] - best)
+    total = jnp.sum(power, axis=1, keepdims=True)
+    mixed = jnp.dot(power.astype(BF), proj[...], preferred_element_type=F32)
+    out_ref[...] = mixed / total
+    lse_ref[...] = jnp.broadcast_to(best + jnp.log(total), lse_ref.shape)
+
+
+def half(tokens, head, proj, in_proj, with_side, limit):
+    n, depth = tokens.shape
+    rows, rank = proj.shape
+    count = 3 if with_side else 2
+    return pl.pallas_call(
+        functools.partial(half_kernel, with_side),
+        in_specs=[pl.BlockSpec(memory_space=pl.ANY)] * 4,
+        out_specs=[pl.BlockSpec(memory_space=pltpu.VMEM)] * count,
+        out_shape=[jax.ShapeDtypeStruct((n, rank), F32)] * count,
+        scratch_shapes=[
+            pltpu.VMEM((n, depth), BF),
+            pltpu.VMEM((rows, depth), BF),
+            pltpu.VMEM((rows, rank), BF),
+            pltpu.VMEM((depth, rank), BF),
+            pltpu.VMEM((n, rows), F32),
+            pltpu.SemaphoreType.DMA((7,)),
+        ],
+        compiler_params=pltpu.CompilerParams(vmem_limit_bytes=limit << 20),
+        cost_estimate=pl.CostEstimate(
+            flops=2 * n * rows * depth, bytes_accessed=rows * depth * 2, transcendentals=0
+        ),
+    )(tokens, head, proj, in_proj)
+
+
 def hot_kernel(where, targets_ref, own_ref, sib_ref, out_ref):
     local = out_ref.shape[1]
     total = jnp.zeros(out_ref.shape, F32)
@@ -228,7 +291,14 @@
 
 def pack_kernel(place, *refs):
     outs, lses, sides = refs[0:3], refs[3:6], refs[6:9]
-    hot_ref, send_ref, side_ref, out_nat, lse_nat = refs[9:]
+    outs, lses = list(outs), list(lses)
+    more_out, more_lse, hot_ref, send_ref, side_ref, out_nat, lse_nat, out_own, lse_own = refs[9:]
+    top = jnp.maximum(lses[0][...], more_lse[...])
+    here = jnp.exp(lses[0][...] - top)
+    there = jnp.exp(more_lse[...] - top)
+    out_own[...] = (outs[0][...] * here + more_out[...] * there) / (here + there)
+    lse_own[...] = top + jnp.log(here + there)
+    outs[0], lses[0] = out_own, lse_own
     k = place[0]
     spot = [place[1], place[2], place[3], place[4]]
 
@@ -270,20 +340,20 @@
             send_ref[to] = jnp.concatenate([mixed[part], hot[part], stats], axis=0).astype(BF)
 
 
-def pack(place, results, hot):
+def pack(place, results, more, hot):
     outs, lses, sides = zip(*results)
     return pl.pallas_call(
         pack_kernel,
         in_specs=[pl.BlockSpec(memory_space=pltpu.SMEM)]
-        + [pl.BlockSpec(memory_space=pltpu.VMEM)] * 10,
+        + [pl.BlockSpec(memory_space=pltpu.VMEM)] * 12,
         out_specs=[pl.BlockSpec(memory_space=pltpu.VMEM)] * 2,
         out_shape=[
             jax.ShapeDtypeStruct((128, 24, 128), BF),
             jax.ShapeDtypeStruct((8, 4, 32, 128), F32),
         ],
-        scratch_shapes=[pltpu.VMEM((8, 4, 32, 128), F32)] * 2,
+        scratch_shapes=[pltpu.VMEM((8, 4, 32, 128), F32)] * 2 + [pltpu.VMEM((256, 128), F32)] * 2,
         compiler_params=pltpu.CompilerParams(vmem_limit_bytes=16 * 1024 * 1024),
-    )(place, *outs, *lses, *sides, hot)
+    )(place, *outs, *lses, *sides, *more, hot)
 
 
 def merge_kernel(got_ref, out_ref):
@@ -435,19 +505,21 @@
     again, local_targets = lax.optimization_barrier((hidden, local_targets))
     mine_d = lax.dynamic_slice_in_dim(again, (3 - k) * 64, 64, 0)
 
-    mine_d, near_a, proj_sib = lax.optimization_barrier((mine_d, near_a, proj_sib))
+    first = half(hidden, out_head, out_proj, in_proj, True, 50)
+    mine_d, near_a, proj_sib, first = lax.optimization_barrier((mine_d, near_a, proj_sib, first))
     near, ahead = rows_of(
         ((0, 0, 64, 0, 0), (1, 0, 64, 0, 64), (0, 0, 64, 1, 0), (2, 0, 64, 1, 64)),
         [near_a, near_b, mine_d],
         [128, 128],
+        pltpu.VMEM,
     )
     near_y = move(near, along_y)
     near_z = move(near, along_z)
     ahead = move(ahead, along_x)
     rest = (out_head, head_sib, out_proj, proj_sib, in_proj)
-    first = flash([hidden], *rest)
-    first, ahead, near_y, near_z = lax.optimization_barrier((first, ahead, near_y, near_z))
-    first, local_targets = lax.optimization_barrier((first, local_targets))
+    more = half(hidden, head_sib, proj_sib, in_proj, False, 24)
+    more, ahead, near_y, near_z = lax.optimization_barrier((more, ahead, near_y, near_z))
+    more, local_targets = lax.optimization_barrier((more, local_targets))
     hot = hot_rows(jnp.stack([first_row, sib_row]), local_targets, out_proj, proj_sib)
     last_y, last_z, far_d = rows_of(
         (
@@ -474,7 +546,7 @@
             (x + 2 + 2 * c) % 4,
         ]
     ).astype(jnp.int32)
-    send, side = pack(place, (first, second, third), hot)
+    send, side = pack(place, (first, second, third), more, hot)
     side_sib = move(side, to_sibling)
 
     got = lax.all_to_all(send, ALL, 0, 0, tiled=True)

time: 120 us -> 130 us (1.083)
  Pallas kernels: 41.4 us -> 56.8 us
  waiting for transfers between devices: 30 us -> 25.5 us
  local copies, waits for them, and re-layouts: 10.9 us -> 9.04 us
    pallas_call x0 -> x2, Pallas kernels: none -> 15.3 us  [half(): pl.pallas_call(functools.partial(half_kernel, with_side), in_specs=[pl.Bl...]
    ppermute x11, waiting for transfers between devices: 8.2 us -> 4.44 us  [move(): return lax.ppermute(value, ALL, pairs)]
    unnamed x16 -> x24, local copies, waits for them, and re-layouts: 7.16 us -> 3.8 us
    pallas_call x3 -> x2, Pallas kernels: 28.1 us -> 24.9 us  [flash(): pl.pallas_call(functools.partial(flash_kernel, sizes, stream), in_specs=[...]
    pallas_call x2, Pallas kernels: 1.6 us -> 4.49 us  [rows_of(): pl.pallas_call(functools.partial(rows_kernel, plan, len(sources)), in_spe...]
  transfers between devices with their start and end apart: 13 -> 13, of which waited for: 5 -> 4; matrix products, arithmetic and copies ran while one was open for 3% -> 4% of each run, Pallas kernels for 21% -> 29%
where the time goes in v2:
time: 130 us; the launch traced here: 129 us
  Pallas kernels  56.8 us (44%)
  starting transfers between devices  27.5 us (21%)
  waiting for transfers between devices  25.5 us (20%)
  blocking collectives  9.5 us (7%)
  local copies, waits for them, and re-layouts  9.04 us (7%)
    pallas_call x2, Pallas kernels, flash(): pl.pallas_call(functools.partial(flash_kernel, sizes, stream), in_specs=[...  24.9 us
    ppermute x11, starting transfers between devices, move(): return lax.ppermute(value, ALL, pairs)  17.3 us
    pallas_call x2, Pallas kernels, half(): pl.pallas_call(functools.partial(half_kernel, with_side), in_specs=[pl.Bl...  15.3 us
    all_to_all x1, waiting for transfers between devices, on_device(): got = lax.all_to_all(send, ALL, 0, 0, tiled=True)  14.7 us
    all_to_all x1, blocking collectives, on_device(): lax.all_to_all(partial, ('x', 'c'), 0, 0, tiled=True)  9.5 us
    pallas_call x1, Pallas kernels, score(): pl.pallas_call(score_kernel, in_specs=[pl.BlockSpec(memory_space=pltpu.SM...  7.19 us
    all_to_all x1, starting transfers between devices, on_device(): got = lax.all_to_all(send, ALL, 0, 0, tiled=True)  6.69 us
    all_to_all x1, waiting for transfers between devices, on_device(): out = lax.all_to_all(merge(got), ('y', 'z'), 0, 0, tiled=True)  6.43 us
  transfers between devices with their start and end apart: 13, of which 4 were waited for; matrix products, arithmetic and copies ran while one was open for 4% of the time, Pallas kernels for 29%

profile of v2, /device:TPU:1, one launch (start us, length us, event | category | flops | bytes accessed | tf_op | source)
XLA Modules:
  0.0 129.5 jit_solution(85146931171468017)
XLA Ops:
  0.0 1.4 %collective-permute-start.3 = (bf16[1024,4096]{1,0:T(8,128)(2,1)}, bf16[1024,4096]{1,0:T(8,128)(2,1)}, u32[]{:S(2)}, u32[]{:S(2)}) collective-permute-start(bf16[1024,4096]{1,0:T(8,128)(2,1)} %refs_3_.1), channel_id=1, source_target_pairs={{0,1},{1,0},{2,3},{3,2},{4,5},{5,4},{6,7},{7,6},{8,9},{9,8},{10,11... | collective-permute-start | bytes 25165832 | tf_op jit(solution)/shard_map/ppermute | solution.py:32
  1.4 1.9 %constant_dynamic-slice_fusion = bf16[64,4096]{1,0:T(8,128)(2,1)} fusion(bf16[256,4096]{1,0:T(8,128)(2,1)} %tok_far.3, s32[]{:T(128)S(6)} %select_n.56), kind=kLoop, calls=%fused_computation.11 | loop fusion | bytes 1048580 | tf_op jit(solution)/shard_map/dynamic_slice | solution.py:489
  3.3 2.6 %collective-permute-start = (bf16[64,4096]{1,0:T(8,128)(2,1)}, bf16[64,4096]{1,0:T(8,128)(2,1)}, u32[]{:S(2)}, u32[]{:S(2)}) collective-permute-start(bf16[64,4096]{1,0:T(8,128)(2,1)} %constant_dynamic-slice_fusion), channel_id=1, source_target_pairs={{0,2},{1,7},{2,4},{3,1},{4,6},{5,3},{6,0},{7,5},{8,10},{9,15},{10,... | collective-permute-start | bytes 1572872 | tf_op jit(solution)/shard_map/ppermute | solution.py:32
  9.1 1.6 %copy-done = bf16[256,4096]{1,0:T(8,128)(2,1)S(1)} copy-done((bf16[256,4096]{1,0:T(8,128)(2,1)S(1)}, bf16[256,4096]{1,0:T(8,128)(2,1)}, u32[]{:S(2)}) %copy-start) | copy-done | bytes 2097176
  10.7 1.2 copy-done.2
  12.9 7.8 %shard_map.73 = (f32[256,128]{1,0:T(8,128)S(1)}, f32[256,128]{1,0:T(8,128)S(1)}, f32[256,128]{1,0:T(8,128)S(1)}) custom-call(bf16[256,4096]{1,0:T(8,128)(2,1)S(1)} %copy-done, bf16[1024,4096]{1,0:T(8,128)(2,1)} %refs_3_.1, bf16[1024,128]{1,0:T(8,128)(2,1)S(1)} %copy-done.4, bf16[4096,128]{1,0:T(8,128)(2,1)S(1)} %copy-done.2), custom_call_target="tpu_custom_call" | custom-call | flops 2147483648 | bytes 8388608 | tf_op jit(solution)/shard_map/pallas_call | solution.py:242
  20.7 2.9 %shard_map.74 = (bf16[128,4096]{1,0:T(8,128)(2,1)}, bf16[128,4096]{1,0:T(8,128)(2,1)}) custom-call(bf16[64,4096]{1,0:T(8,128)(2,1)} %collective-permute-done.refs_0_, bf16[64,4096]{1,0:T(8,128)(2,1)} %collective-permute-done.2.refs_1_, bf16[64,4096]{1,0:T(8,128)(2,1)S(1)} %constant_dynamic-slice_fusion.1.refs_2_), custom_call_target="tpu_custom_call" | custom-call | bytes 4194304 | tf_op jit(solution)/shard_map/pallas_call | solution.py:74
  24.5 2.7 %collective-permute-start.5 = (bf16[128,4096]{1,0:T(8,128)(2,1)}, bf16[128,4096]{1,0:T(8,128)(2,1)}, u32[]{:S(2)}, u32[]{:S(2)}) collective-permute-start(bf16[128,4096]{1,0:T(8,128)(2,1)} %get-tuple-element.46.refs_0_), channel_id=1, source_target_pairs={{0,32},{1,97},{2,34},{3,99},{4,36},{5,101},{6,38},{7,103},{8,40},{... | collective-permute-start | bytes 3145736 | tf_op jit(solution)/shard_map/ppermute | solution.py:32
  27.3 3.8 %collective-permute-start.6 = (bf16[128,4096]{1,0:T(8,128)(2,1)}, bf16[128,4096]{1,0:T(8,128)(2,1)}, u32[]{:S(2)}, u32[]{:S(2)}) collective-permute-start(bf16[128,4096]{1,0:T(8,128)(2,1)} %get-tuple-element.46.refs_0_), channel_id=1, source_target_pairs={{0,8},{1,25},{2,10},{3,27},{4,12},{5,29},{6,14},{7,31},{8,16},{9,1... | collective-permute-start | bytes 3145736 | tf_op jit(solution)/shard_map/ppermute | solution.py:32
  31.2 7.4 %shard_map.75 = (f32[256,128]{1,0:T(8,128)S(1)}, f32[256,128]{1,0:T(8,128)S(1)}) custom-call(bf16[256,4096]{1,0:T(8,128)(2,1)S(1)} %copy-done.1, bf16[1024,4096]{1,0:T(8,128)(2,1)} %collective-permute-done.3.head_far.refs_5_.refs_4_, bf16[1024,128]{1,0:T(8,128)(2,1)} %collective-permute-done.1.proj_far.refs_7_.refs_6_.sib_ref, bf16[4096,128]{1,0:T(8,128)(2,1)S(1)} %copy-done.3), custom_call_target="tpu_custom_call" | custom-call | flops 2147483648 | bytes 8388608 | tf_op jit(solution)/shard_map/pallas_call | solution.py:242
  39.3 3.8 %collective-permute-done.6.refs_2_ = bf16[128,4096]{1,0:T(8,128)(2,1)} collective-permute-done((bf16[128,4096]{1,0:T(8,128)(2,1)}, bf16[128,4096]{1,0:T(8,128)(2,1)}, u32[]{:S(2)}, u32[]{:S(2)}) %collective-permute-start.6) | collective-permute-done | bytes 1048608 | tf_op jit(solution)/shard_map/ppermute | solution.py:32
  43.1 1.6 %shard_map.77 = (bf16[96,4096]{1,0:T(8,128)(2,1)S(1)}, bf16[96,4096]{1,0:T(8,128)(2,1)S(1)}, bf16[64,4096]{1,0:T(8,128)(2,1)S(1)}) custom-call(bf16[128,4096]{1,0:T(8,128)(2,1)} %collective-permute-done.4.refs_3_.refs_0_, bf16[128,4096]{1,0:T(8,128)(2,1)} %collective-permute-done.5.refs_1_, bf16[128,4096]{1,0:T(8,128)(2,1)} %collective-permute-done.6.refs_2_), custom_call_target="tpu_custom_call" | custom-call | bytes 4194304 | tf_op jit(solution)/shard_map/pallas_call | solution.py:74
  45.2 3.1 %collective-permute-start.8 = (bf16[96,4096]{1,0:T(8,128)(2,1)S(1)}, bf16[96,4096]{1,0:T(8,128)(2,1)S(1)}, u32[]{:S(2)}, u32[]{:S(2)}) collective-permute-start(bf16[96,4096]{1,0:T(8,128)(2,1)S(1)} %get-tuple-element.56), channel_id=1, source_target_pairs={{0,8},{1,25},{2,10},{3,27},{4,12},{5,29},{6,14},{7,31},{8,16},{9,1... | collective-permute-start | bytes 2359304 | tf_op jit(solution)/shard_map/ppermute | solution.py:32
  48.6 1.7 %shard_map.79.refs_11_ = f32[128,1024]{1,0:T(8,128)S(1)} custom-call(s32[2]{0:T(128)S(1)} %pad_add_fusion.where, s32[1,1024]{1,0:T(1,128)S(1)} %reshape.44.targets_ref, bf16[1024,128]{1,0:T(8,128)(2,1)S(1)} %copy-done.5, bf16[1024,128]{1,0:T(8,128)(2,1)} %collective-permute-done.1.proj_far.refs_7_.refs_6_.sib_ref), custom_call_target="tpu_custom_call" | custom-call | flops 536870912 | bytes 1048576 | tf_op jit(solution)/shard_map/pallas_call | solution.py:280
  50.3 16.7 %shard_map.76 = (f32[512,128]{1,0:T(8,128)S(1)}, f32[512,128]{1,0:T(8,128)S(1)}, f32[512,128]{1,0:T(8,128)S(1)}) custom-call(bf16[128,4096]{1,0:T(8,128)(2,1)} %get-tuple-element.46.refs_0_, bf16[128,4096]{1,0:T(8,128)(2,1)} %collective-permute-done.5.refs_1_, bf16[128,4096]{1,0:T(8,128)(2,1)} %collective-permute-done.6.refs_2_, ...), custom_call_target="tpu_custom_call" | custom-call | flops 8589934592 | bytes 4194304 | tf_op jit(solution)/shard_map/pallas_call | solution.py:179
  67.1 8.2 %shard_map.78 = (f32[256,128]{1,0:T(8,128)S(1)}, f32[256,128]{1,0:T(8,128)S(1)}, f32[256,128]{1,0:T(8,128)S(1)}) custom-call(bf16[96,4096]{1,0:T(8,128)(2,1)S(1)} %collective-permute-done.7.refs_0_, bf16[96,4096]{1,0:T(8,128)(2,1)S(1)} %collective-permute-done.8.refs_1_, bf16[64,4096]{1,0:T(8,128)(2,1)S(1)} %collective-permute-done.9.refs_2_, ...), custom_call_target="tpu_custom_call" | custom-call | flops 4294967296 | bytes 2097152 | tf_op jit(solution)/shard_map/pallas_call | solution.py:179
  75.3 1.9 %shard_map.80 = (bf16[128,24,128]{2,1,0:T(8,128)(2,1)}, f32[8,4,32,128]{3,2,1,0:T(8,128)S(1)}) custom-call(s32[5]{0:T(128)S(1)} %stack.38.place, f32[256,128]{1,0:T(8,128)S(1)} %get-tuple-element.43.refs_0_, f32[512,128]{1,0:T(8,128)S(1)} %get-tuple-element.54.refs_1_, f32[256,128]{1,0:T(8,128)S(1)} %get-tuple-element.58.refs_2_, f32[256,128]{1,0:T(8,128)S(1)} %copy-done.7, ...), custom_call_target="tpu_custom_call" | custom-call | tf_op jit(solution)/shard_map/pallas_call | solution.py:345
  77.2 6.7 %all-to-all-start = ((bf16[128,24,128]{2,1,0:T(8,128)(2,1)}), bf16[128,24,128]{2,1,0:T(8,128)(2,1)S(1)}, u32[]{:S(2)}, u32[]{:S(2)}) async-start(bf16[128,24,128]{2,1,0:T(8,128)(2,1)} %get-tuple-element.71), calls=%async_computation | async-start | bytes 1572864 | tf_op jit(solution)/shard_map/all_to_all | solution.py:552
  85.7 14.7 %all-to-all-done.got_ref = bf16[128,24,128]{2,1,0:T(8,128)(2,1)S(1)} async-done(((bf16[128,24,128]{2,1,0:T(8,128)(2,1)}), bf16[128,24,128]{2,1,0:T(8,128)(2,1)S(1)}, u32[]{:S(2)}, u32[]{:S(2)}) %all-to-all-start) | async-done | bytes 786464 | tf_op jit(solution)/shard_map/all_to_all | solution.py:552
  100.4 1.5 %shard_map.81 = f32[16,8,256]{2,1,0:T(8,128)} custom-call(bf16[128,24,128]{2,1,0:T(8,128)(2,1)S(1)} %all-to-all-done.got_ref), custom_call_target="tpu_custom_call" | custom-call | tf_op jit(solution)/shard_map/pallas_call | solution.py:385
  101.9 3.5 %all-to-all-start.1 = ((f32[16,8,256]{2,1,0:T(8,128)}), f32[16,8,256]{2,1,0:T(8,128)S(1)}, u32[]{:S(2)}, u32[]{:S(2)}) async-start(f32[16,8,256]{2,1,0:T(8,128)} %shard_map.81), calls=%async_computation.1 | async-start | bytes 262144 | tf_op jit(solution)/shard_map/all_to_all | solution.py:554
  105.7 6.4 %all-to-all-done.1.out_ref = f32[16,8,256]{2,1,0:T(8,128)S(1)} async-done(((f32[16,8,256]{2,1,0:T(8,128)}), f32[16,8,256]{2,1,0:T(8,128)S(1)}, u32[]{:S(2)}, u32[]{:S(2)}) %all-to-all-start.1) | async-done | bytes 131104 | tf_op jit(solution)/shard_map/all_to_all | solution.py:554
  112.2 7.2 %shard_map.82 = f32[8,16,256]{2,1,0:T(8,128)S(1)} custom-call(s32[4]{0:T(128)S(1)} %get-tuple-element.78.flags, f32[16,8,256]{2,1,0:T(8,128)S(1)} %all-to-all-done.1.out_ref, f32[8,4,32,128]{3,2,1,0:T(8,128)S(1)} %get-tuple-element.72.own_hbm, f32[8,4,32,128]{3,2,1,0:T(8,128)S(1)} %collective-permute-done.10.sib_hbm, s32[8,256]{1,0:T(8,128)S(1)} %reshape.46.seq_ref, ...), custom_call_target="tpu_custom_call" | custom-call | tf_op jit(solution)/shard_map/pallas_call | solution.py:455
  119.4 9.5 %all_to_all.15 = f32[8,16,256]{2,1,0:T(8,128)S(1)} all-to-all(f32[8,16,256]{2,1,0:T(8,128)S(1)} %shard_map.82), channel_id=1, replica_groups=mesh['y'=4,'z'=4,'x'=4,'c'=2] {'x','c'}, dimensions={0} | all-to-all | bytes 262144 | tf_op jit(solution)/shard_map/all_to_all | solution.py:556
  (62 shorter events, 9.5 us)
Async XLA Ops:
  0.0 31.2 %copy-start.1 = (bf16[256,4096]{1,0:T(8,128)(2,1)S(1)}, bf16[256,4096]{1,0:T(8,128)(2,1)}, u32[]{:S(2)}) copy-start(bf16[256,4096]{1,0:T(8,128)(2,1)} %tok_far.3) | copy-start | bytes 6291460
  0.0 31.2 %collective-permute-start.3 = (bf16[1024,4096]{1,0:T(8,128)(2,1)}, bf16[1024,4096]{1,0:T(8,128)(2,1)}, u32[]{:S(2)}, u32[]{:S(2)}) collective-permute-start(bf16[1024,4096]{1,0:T(8,128)(2,1)} %refs_3_.1), channel_id=1, source_target_pairs={{0,1},{1,0},{2,3},{3,2},{4,5},{5,4},{6,7},{7,6},{8,9},{9,8},{10,11... | collective-permute-start | bytes 25165832 | tf_op jit(solution)/shard_map/ppermute | solution.py:32
  3.3 17.4 %collective-permute-start = (bf16[64,4096]{1,0:T(8,128)(2,1)}, bf16[64,4096]{1,0:T(8,128)(2,1)}, u32[]{:S(2)}, u32[]{:S(2)}) collective-permute-start(bf16[64,4096]{1,0:T(8,128)(2,1)} %constant_dynamic-slice_fusion), channel_id=1, source_target_pairs={{0,2},{1,7},{2,4},{3,1},{4,6},{5,3},{6,0},{7,5},{8,10},{9,15},{10,... | collective-permute-start | bytes 1572872 | tf_op jit(solution)/shard_map/ppermute | solution.py:32
  5.9 14.8 %collective-permute-start.2 = (bf16[64,4096]{1,0:T(8,128)(2,1)}, bf16[64,4096]{1,0:T(8,128)(2,1)}, u32[]{:S(2)}, u32[]{:S(2)}) collective-permute-start(bf16[64,4096]{1,0:T(8,128)(2,1)} %constant_dynamic-slice_fusion), channel_id=1, source_target_pairs={{0,7},{1,2},{2,1},{3,4},{4,3},{5,6},{6,5},{7,0},{8,15},{9,10},{10,... | collective-permute-start | bytes 1572872 | tf_op jit(solution)/shard_map/ppermute | solution.py:32
  6.2 14.6 %collective-permute-start.1 = (bf16[1024,128]{1,0:T(8,128)(2,1)}, bf16[1024,128]{1,0:T(8,128)(2,1)}, u32[]{:S(2)}, u32[]{:S(2)}) collective-permute-start(bf16[1024,128]{1,0:T(8,128)(2,1)} %own_ref.1), channel_id=1, source_target_pairs={{0,1},{1,0},{2,3},{3,2},{4,5},{5,4},{6,7},{7,6},{8,9},{9,8},{10,11... | collective-permute-start | bytes 786440 | tf_op jit(solution)/shard_map/ppermute | solution.py:32
  9.1 1.6 %copy-start = (bf16[256,4096]{1,0:T(8,128)(2,1)S(1)}, bf16[256,4096]{1,0:T(8,128)(2,1)}, u32[]{:S(2)}) copy-start(bf16[256,4096]{1,0:T(8,128)(2,1)} %tok_far.3) | copy-start | bytes 6291460
  10.7 1.2 copy-start.2
  12.9 18.3 %copy-start.3 = (bf16[4096,128]{1,0:T(8,128)(2,1)S(1)}, bf16[4096,128]{1,0:T(8,128)(2,1)}, u32[]{:S(2)}) copy-start(bf16[4096,128]{1,0:T(8,128)(2,1)} %refs_7_.1) | copy-start | bytes 3145732
  20.7 3.0 %copy-start.6 = (f32[256,128]{1,0:T(8,128)}, f32[256,128]{1,0:T(8,128)S(1)}, u32[]{:S(2)}) copy-start(f32[256,128]{1,0:T(8,128)S(1)} %get-tuple-element.59.refs_3_) | copy-start | bytes 393220
  20.7 3.0 %copy-start.8 = (f32[256,128]{1,0:T(8,128)}, f32[256,128]{1,0:T(8,128)S(1)}, u32[]{:S(2)}) copy-start(f32[256,128]{1,0:T(8,128)S(1)} %get-tuple-element.62.refs_6_) | copy-start | bytes 393220
  20.7 27.9 %copy-start.5 = (bf16[1024,128]{1,0:T(8,128)(2,1)S(1)}, bf16[1024,128]{1,0:T(8,128)(2,1)}, u32[]{:S(2)}) copy-start(bf16[1024,128]{1,0:T(8,128)(2,1)} %own_ref.1) | copy-start | bytes 786436
  23.7 15.0 %collective-permute-start.4 = (bf16[128,4096]{1,0:T(8,128)(2,1)}, bf16[128,4096]{1,0:T(8,128)(2,1)}, u32[]{:S(2)}, u32[]{:S(2)}) collective-permute-start(bf16[128,4096]{1,0:T(8,128)(2,1)} %get-tuple-element.50), channel_id=1, source_target_pairs={{0,2},{1,7},{2,4},{3,1},{4,6},{5,3},{6,0},{7,5},{8,10},{9,15},{10,... | collective-permute-start | bytes 3145736 | tf_op jit(solution)/shard_map/ppermute | solution.py:32
  24.5 14.8 %collective-permute-start.5 = (bf16[128,4096]{1,0:T(8,128)(2,1)}, bf16[128,4096]{1,0:T(8,128)(2,1)}, u32[]{:S(2)}, u32[]{:S(2)}) collective-permute-start(bf16[128,4096]{1,0:T(8,128)(2,1)} %get-tuple-element.46.refs_0_), channel_id=1, source_target_pairs={{0,32},{1,97},{2,34},{3,99},{4,36},{5,101},{6,38},{7,103},{8,40},{... | collective-permute-start | bytes 3145736 | tf_op jit(solution)/shard_map/ppermute | solution.py:32
  27.3 15.8 %collective-permute-start.6 = (bf16[128,4096]{1,0:T(8,128)(2,1)}, bf16[128,4096]{1,0:T(8,128)(2,1)}, u32[]{:S(2)}, u32[]{:S(2)}) collective-permute-start(bf16[128,4096]{1,0:T(8,128)(2,1)} %get-tuple-element.46.refs_0_), channel_id=1, source_target_pairs={{0,8},{1,25},{2,10},{3,27},{4,12},{5,29},{6,14},{7,31},{8,16},{9,1... | collective-permute-start | bytes 3145736 | tf_op jit(solution)/shard_map/ppermute | solution.py:32
  31.1 19.2 %slice-start = ((s8[8388608]{0:T(1024)(128)(4,1)}), s8[4194304]{0:T(1024)(128)(4,1)S(1)}, s32[]{:S(2)}) async-start(s8[8388608]{0:T(1024)(128)(4,1)} %bitcast.12), calls=%async_computation.3 | async-start | bytes 8388608
  31.2 19.1 %slice-start.1 = ((s8[8388608]{0:T(1024)(128)(4,1)}), s8[4194304]{0:T(1024)(128)(4,1)S(1)}, s32[]{:S(2)}) async-start(s8[8388608]{0:T(1024)(128)(4,1)} %bitcast.12), calls=%async_computation.4 | async-start | bytes 8388608
  44.7 22.4 %collective-permute-start.7 = (bf16[96,4096]{1,0:T(8,128)(2,1)S(1)}, bf16[96,4096]{1,0:T(8,128)(2,1)S(1)}, u32[]{:S(2)}, u32[]{:S(2)}) collective-permute-start(bf16[96,4096]{1,0:T(8,128)(2,1)S(1)} %get-tuple-element.55), channel_id=1, source_target_pairs={{0,32},{1,97},{2,34},{3,99},{4,36},{5,101},{6,38},{7,103},{8,40},{... | collective-permute-start | bytes 2359304 | tf_op jit(solution)/shard_map/ppermute | solution.py:32
  45.2 21.9 %collective-permute-start.8 = (bf16[96,4096]{1,0:T(8,128)(2,1)S(1)}, bf16[96,4096]{1,0:T(8,128)(2,1)S(1)}, u32[]{:S(2)}, u32[]{:S(2)}) collective-permute-start(bf16[96,4096]{1,0:T(8,128)(2,1)S(1)} %get-tuple-element.56), channel_id=1, source_target_pairs={{0,8},{1,25},{2,10},{3,27},{4,12},{5,29},{6,14},{7,31},{8,16},{9,1... | collective-permute-start | bytes 2359304 | tf_op jit(solution)/shard_map/ppermute | solution.py:32
  48.3 18.7 %collective-permute-start.9 = (bf16[64,4096]{1,0:T(8,128)(2,1)S(1)}, bf16[64,4096]{1,0:T(8,128)(2,1)S(1)}, u32[]{:S(2)}, u32[]{:S(2)}) collective-permute-start(bf16[64,4096]{1,0:T(8,128)(2,1)S(1)} %get-tuple-element.57), channel_id=1, source_target_pairs={{0,2},{1,7},{2,4},{3,1},{4,6},{5,3},{6,0},{7,5},{8,10},{9,15},{10,... | collective-permute-start | bytes 1572872 | tf_op jit(solution)/shard_map/ppermute | solution.py:32
  67.0 8.2 %copy-start.7 = (f32[256,128]{1,0:T(8,128)S(1)}, f32[256,128]{1,0:T(8,128)}, u32[]{:S(2)}) copy-start(f32[256,128]{1,0:T(8,128)} %copy-done.6) | copy-start | bytes 393220
  67.1 8.2 %copy-start.9 = (f32[256,128]{1,0:T(8,128)S(1)}, f32[256,128]{1,0:T(8,128)}, u32[]{:S(2)}) copy-start(f32[256,128]{1,0:T(8,128)} %copy-done.8) | copy-start | bytes 393220
  77.2 23.2 %all-to-all-start = ((bf16[128,24,128]{2,1,0:T(8,128)(2,1)}), bf16[128,24,128]{2,1,0:T(8,128)(2,1)S(1)}, u32[]{:S(2)}, u32[]{:S(2)}) async-start(bf16[128,24,128]{2,1,0:T(8,128)(2,1)} %get-tuple-element.71), calls=%async_computation | async-start | bytes 1572864 | tf_op jit(solution)/shard_map/all_to_all | solution.py:552
  83.9 21.9 %collective-permute-start.10 = (f32[8,4,32,128]{3,2,1,0:T(8,128)S(1)}, f32[8,4,32,128]{3,2,1,0:T(8,128)S(1)}, u32[]{:S(2)}, u32[]{:S(2)}) collective-permute-start(f32[8,4,32,128]{3,2,1,0:T(8,128)S(1)} %get-tuple-element.72.own_hbm), channel_id=1, source_target_pairs={{0,1},{1,0},{2,3},{3,2},{4,5},{5,4},{6,7},{7,6},{8,9},{9,8},{10,11... | collective-permute-start | bytes 1572872 | tf_op jit(solution)/shard_map/ppermute | solution.py:32
  101.9 10.3 %all-to-all-start.1 = ((f32[16,8,256]{2,1,0:T(8,128)}), f32[16,8,256]{2,1,0:T(8,128)S(1)}, u32[]{:S(2)}, u32[]{:S(2)}) async-start(f32[16,8,256]{2,1,0:T(8,128)} %shard_map.81), calls=%async_computation.1 | async-start | bytes 262144 | tf_op jit(solution)/shard_map/all_to_all | solution.py:554
  (1 other events, 0.9 us)

commit v3 on v1

--- a/solution.py
+++ b/solution.py
@@ -122,45 +122,42 @@
 
     dims = (((1,), (1,)), ((), ()))
     tile = 1024 if tok.shape[0] <= 256 else 512
-    if not stream:
-        for low in range(0, rows, tile):
-            scores[:, low : low + tile] = lax.dot_general(
-                tok[...], heads[0][low : low + tile, :], dims, preferred_element_type=F32
-            )
-        for block in blocks:
-            block.wait()
-        for low in range(0, rows, tile):
-            scores[:, rows + low : rows + low + tile] = lax.dot_general(
-                tok[...], held[low : low + tile, :], dims, preferred_element_type=F32
-            )
-    else:
-        for n, block in enumerate(blocks):
-            block.wait()
-            if n + AHEAD < len(blocks):
-                blocks[n + AHEAD].start()
-            low, high = bounds[n], bounds[n + 1]
-            scores[:, low:high] = lax.dot_general(
-                tok[...], held[low:high, :], dims, preferred_element_type=F32
-            )
-    for copy in others:
-        copy.wait()
+    step = 512
+
+    def softmax_part(which):
+        first, last = which * rows, (which + 1) * rows
+        best = scores[:, first : first + step]
+        for low in range(first + step, last, step):
+            best = jnp.maximum(best, scores[:, low : low + step])
+        best = jnp.max(best, axis=1, keepdims=True)
+        total = None
+        mixed = None
+        for low in range(first, last, step):
+            power = jnp.exp(scores[:, low : low + step] - best)
+            total = power if low == first else total + power
+            proj = projs[which][low - first : low - first + step, :]
+            part = jnp.dot(power.astype(BF), proj, preferred_element_type=F32)
+            mixed = part if low == first else mixed + part
+        return best, jnp.sum(total, axis=1, keepdims=True), mixed
+
+    for low in range(0, rows, tile):
+        scores[:, low : low + tile] = lax.dot_general(
+            tok[...], heads[0][low : low + tile, :], dims, preferred_element_type=F32
+        )
+    for block in blocks:
+        block.wait()
+    best_a, total_a, mixed_a = softmax_part(0)
+    for low in range(0, rows, tile):
+        scores[:, rows + low : rows + low + tile] = lax.dot_general(
+            tok[...], held[low : low + tile, :], dims, preferred_element_type=F32
+        )
     side_ref[...] = jnp.dot(tok[...], in_ref[...], preferred_element_type=F32)
-
-    step = 512
-    best = scores[:, 0:step]
-    for low in range(step, 2 * rows, step):
-        best = jnp.maximum(best, scores[:, low : low + step])
-    best = jnp.max(best, axis=1, keepdims=True)
-    total = None
-    mixed = None
-    for low in range(0, 2 * rows, step):
-        power = jnp.exp(scores[:, low : low + step] - best)
-        total = power if low == 0 else total + power
-        proj = projs[low // rows][low % rows : low % rows + step, :]
-        part = jnp.dot(power.astype(BF), proj, preferred_element_type=F32)
-        mixed = part if low == 0 else mixed + part
-    total = jnp.sum(total, axis=1, keepdims=True)
-    out_ref[...] = mixed / total
+    best_b, total_b, mixed_b = softmax_part(1)
+    best = jnp.maximum(best_a, best_b)
+    scale_a = jnp.exp(best_a - best)
+    scale_b = jnp.exp(best_b - best)
+    total = total_a * scale_a + total_b * scale_b
+    out_ref[...] = (mixed_a * scale_a + mixed_b * scale_b) / total
     lse_ref[...] = jnp.broadcast_to(best + jnp.log(total), lse_ref.shape)
 
 

time: 120 us -> 120 us (level)
  no operation moved by 1% of the time
where the time goes in v3:
time: 120 us; the launch traced here: 119 us
  Pallas kernels  40.9 us (34%)
  waiting for transfers between devices  30 us (25%)
  starting transfers between devices  27.2 us (23%)
  local copies, waits for them, and re-layouts  10.9 us (9%)
  blocking collectives  9.5 us (8%)
    pallas_call x3, Pallas kernels, flash(): pl.pallas_call(functools.partial(flash_kernel, sizes, stream), in_specs=[...  27.7 us
    ppermute x11, starting transfers between devices, move(): return lax.ppermute(value, ALL, pairs)  17.4 us
    all_to_all x1, waiting for transfers between devices, on_device(): got = lax.all_to_all(send, ALL, 0, 0, tiled=True)  15.3 us
    all_to_all x1, blocking collectives, on_device(): lax.all_to_all(partial, ('x', 'c'), 0, 0, tiled=True)  9.5 us
    ppermute x11, waiting for transfers between devices, move(): return lax.ppermute(value, ALL, pairs)  8.2 us
    pallas_call x1, Pallas kernels, score(): pl.pallas_call(score_kernel, in_specs=[pl.BlockSpec(memory_space=pltpu.SM...  7.19 us
    unnamed x16, local copies, waits for them, and re-layouts  7.16 us
    all_to_all x1, waiting for transfers between devices, on_device(): out = lax.all_to_all(merge(got), ('y', 'z'), 0, 0, tiled=True)  6.43 us
  transfers between devices with their start and end apart: 13, of which 5 were waited for; matrix products, arithmetic and copies ran while one was open for 3% of the time, Pallas kernels for 21%

profile of v3, /device:TPU:1, one launch (start us, length us, event | category | flops | bytes accessed | tf_op | source)
XLA Modules:
  0.0 119.5 jit_solution(14151900062788891233)
XLA Ops:
  0.0 1.4 %collective-permute-start = (bf16[1024,4096]{1,0:T(8,128)(2,1)}, bf16[1024,4096]{1,0:T(8,128)(2,1)}, u32[]{:S(2)}, u32[]{:S(2)}) collective-permute-start(bf16[1024,4096]{1,0:T(8,128)(2,1)} %refs_3_.3), channel_id=1, source_target_pairs={{0,1},{1,0},{2,3},{3,2},{4,5},{5,4},{6,7},{7,6},{8,9},{9,8},{10,11... | collective-permute-start | bytes 25165832 | tf_op jit(solution)/shard_map/ppermute | solution.py:32
  2.5 2.6 %collective-permute-start.1 = (bf16[64,4096]{1,0:T(8,128)(2,1)S(1)}, bf16[64,4096]{1,0:T(8,128)(2,1)S(1)}, u32[]{:S(2)}, u32[]{:S(2)}) collective-permute-start(bf16[64,4096]{1,0:T(8,128)(2,1)S(1)} %constant_dynamic-slice_fusion), channel_id=1, source_target_pairs={{0,2},{1,7},{2,4},{3,1},{4,6},{5,3},{6,0},{7,5},{8,10},{9,15},{10,... | collective-permute-start | bytes 1572872 | tf_op jit(solution)/shard_map/ppermute | solution.py:32
  7.2 1.1 constant_dynamic-slice_fusion.1.refs_2_
  8.3 6.5 %collective-permute-done.2.refs_4_.refs_7_.refs_6_.sib_ref = bf16[1024,128]{1,0:T(8,128)(2,1)S(1)} collective-permute-done((bf16[1024,128]{1,0:T(8,128)(2,1)}, bf16[1024,128]{1,0:T(8,128)(2,1)S(1)}, u32[]{:S(2)}, u32[]{:S(2)}) %collective-permute-start.2) | collective-permute-done | bytes 262176 | tf_op jit(solution)/shard_map/ppermute | solution.py:32
  16.5 1.4 %shard_map.74 = (bf16[128,4096]{1,0:T(8,128)(2,1)}, bf16[128,4096]{1,0:T(8,128)(2,1)}) custom-call(bf16[64,4096]{1,0:T(8,128)(2,1)S(1)} %collective-permute-done.1.refs_0_, bf16[64,4096]{1,0:T(8,128)(2,1)S(1)} %collective-permute-done.3.refs_1_, bf16[64,4096]{1,0:T(8,128)(2,1)S(1)} %constant_dynamic-slice_fusion.1.refs_2_), custom_call_target="tpu_custom_call" | custom-call | bytes 4194304 | tf_op jit(solution)/shard_map/pallas_call | solution.py:74
  17.9 3.5 %collective-permute-start.4 = (bf16[128,4096]{1,0:T(8,128)(2,1)}, bf16[128,4096]{1,0:T(8,128)(2,1)S(1)}, u32[]{:S(2)}, u32[]{:S(2)}) collective-permute-start(bf16[128,4096]{1,0:T(8,128)(2,1)} %get-tuple-element.43), channel_id=1, source_target_pairs={{0,2},{1,7},{2,4},{3,1},{4,6},{5,3},{6,0},{7,5},{8,10},{9,15},{10,... | collective-permute-start | bytes 3145736 | tf_op jit(solution)/shard_map/ppermute | solution.py:32
  21.5 2.7 %collective-permute-start.5 = (bf16[128,4096]{1,0:T(8,128)(2,1)}, bf16[128,4096]{1,0:T(8,128)(2,1)S(1)}, u32[]{:S(2)}, u32[]{:S(2)}) collective-permute-start(bf16[128,4096]{1,0:T(8,128)(2,1)} %get-tuple-element.44.refs_0_), channel_id=1, source_target_pairs={{0,32},{1,97},{2,34},{3,99},{4,36},{5,101},{6,38},{7,103},{8,40},{... | collective-permute-start | bytes 3145736 | tf_op jit(solution)/shard_map/ppermute | solution.py:32
  24.2 3.8 %collective-permute-start.6 = (bf16[128,4096]{1,0:T(8,128)(2,1)}, bf16[128,4096]{1,0:T(8,128)(2,1)S(1)}, u32[]{:S(2)}, u32[]{:S(2)}) collective-permute-start(bf16[128,4096]{1,0:T(8,128)(2,1)} %get-tuple-element.44.refs_0_), channel_id=1, source_target_pairs={{0,8},{1,25},{2,10},{3,27},{4,12},{5,29},{6,14},{7,31},{8,16},{9,1... | collective-permute-start | bytes 3145736 | tf_op jit(solution)/shard_map/ppermute | solution.py:32
  28.1 3.4 %copy-done = bf16[1024,4096]{1,0:T(8,128)(2,1)S(1)} copy-done((bf16[1024,4096]{1,0:T(8,128)(2,1)S(1)}, bf16[1024,4096]{1,0:T(8,128)(2,1)}, u32[]{:S(2)}) %copy-start) | copy-done | bytes 8388632
  31.5 1.6 %copy-done.2 = bf16[256,4096]{1,0:T(8,128)(2,1)S(1)} copy-done((bf16[256,4096]{1,0:T(8,128)(2,1)S(1)}, bf16[256,4096]{1,0:T(8,128)(2,1)}, u32[]{:S(2)}) %copy-start.2) | copy-done | bytes 2097176
  33.1 1.2 %copy-done.3 = bf16[4096,128]{1,0:T(8,128)(2,1)S(1)} copy-done((bf16[4096,128]{1,0:T(8,128)(2,1)S(1)}, bf16[4096,128]{1,0:T(8,128)(2,1)}, u32[]{:S(2)}) %copy-start.3) | copy-done | bytes 1048600
  35.3 7.1 %shard_map.73 = (f32[256,128]{1,0:T(8,128)S(1)}, f32[256,128]{1,0:T(8,128)S(1)}, f32[256,128]{1,0:T(8,128)S(1)}) custom-call(bf16[256,4096]{1,0:T(8,128)(2,1)S(1)} %copy-done.2, bf16[1024,4096]{1,0:T(8,128)(2,1)S(1)} %copy-done, bf16[1024,4096]{1,0:T(8,128)(2,1)} %collective-permute-done.refs_2_.refs_5_.refs_4_, bf16[1024,128]{1,0:T(8,128)(2,1)S(1)} %copy-done.5, ...), custom_call_target="tpu_custom_call" | custom-call | flops 4294967296 | bytes 2097152 | tf_op jit(solution)/shard_map/pallas_call | solution.py:176
  43.9 1.3 %shard_map.78.refs_9_ = f32[128,1024]{1,0:T(8,128)S(1)} custom-call(s32[2]{0:T(128)S(1)} %pad_add_fusion.where, s32[1,1024]{1,0:T(1,128)S(1)} %reshape.44.targets_ref, bf16[1024,128]{1,0:T(8,128)(2,1)S(1)} %copy-done.5, bf16[1024,128]{1,0:T(8,128)(2,1)S(1)} %collective-permute-done.2.refs_4_.refs_7_.refs_6_.sib_ref), custom_call_target="tpu_custom_call" | custom-call | flops 536870912 | bytes 1048576 | tf_op jit(solution)/shard_map/pallas_call | solution.py:214
  45.2 13.3 %shard_map.75 = (f32[512,128]{1,0:T(8,128)S(1)}, f32[512,128]{1,0:T(8,128)S(1)}, f32[512,128]{1,0:T(8,128)S(1)}) custom-call(bf16[128,4096]{1,0:T(8,128)(2,1)} %get-tuple-element.44.refs_0_, bf16[128,4096]{1,0:T(8,128)(2,1)S(1)} %collective-permute-done.5.refs_1_, bf16[128,4096]{1,0:T(8,128)(2,1)S(1)} %collective-permute-done.6.refs_2_, ...), custom_call_target="tpu_custom_call" | custom-call | flops 8589934592 | bytes 4194304 | tf_op jit(solution)/shard_map/pallas_call | solution.py:176
  58.5 7.2 %shard_map.77 = (f32[256,128]{1,0:T(8,128)S(1)}, f32[256,128]{1,0:T(8,128)S(1)}, f32[256,128]{1,0:T(8,128)S(1)}) custom-call(bf16[96,4096]{1,0:T(8,128)(2,1)S(1)} %collective-permute-done.7.refs_0_, bf16[96,4096]{1,0:T(8,128)(2,1)S(1)} %collective-permute-done.8.refs_1_, bf16[64,4096]{1,0:T(8,128)(2,1)S(1)} %collective-permute-done.9.refs_2_, ...), custom_call_target="tpu_custom_call" | custom-call | flops 4294967296 | bytes 2097152 | tf_op jit(solution)/shard_map/pallas_call | solution.py:176
  65.8 1.8 %shard_map.79 = (bf16[128,24,128]{2,1,0:T(8,128)(2,1)}, f32[8,4,32,128]{3,2,1,0:T(8,128)S(1)}) custom-call(s32[5]{0:T(128)S(1)} %stack.38.place, f32[256,128]{1,0:T(8,128)S(1)} %get-tuple-element.49.refs_0_, f32[512,128]{1,0:T(8,128)S(1)} %get-tuple-element.53.refs_1_, f32[256,128]{1,0:T(8,128)S(1)} %get-tuple-element.57.refs_2_, ...), custom_call_target="tpu_custom_call" | custom-call | tf_op jit(solution)/shard_map/pallas_call | solution.py:272
  67.5 6.3 %all-to-all-start = ((bf16[128,24,128]{2,1,0:T(8,128)(2,1)}), bf16[128,24,128]{2,1,0:T(8,128)(2,1)S(1)}, u32[]{:S(2)}, u32[]{:S(2)}) async-start(bf16[128,24,128]{2,1,0:T(8,128)(2,1)} %get-tuple-element.65), calls=%async_computation | async-start | bytes 1572864 | tf_op jit(solution)/shard_map/all_to_all | solution.py:477
  73.9 1.1 collective-permute-start.10
  75.1 15.3 %all-to-all-done.got_ref = bf16[128,24,128]{2,1,0:T(8,128)(2,1)S(1)} async-done(((bf16[128,24,128]{2,1,0:T(8,128)(2,1)}), bf16[128,24,128]{2,1,0:T(8,128)(2,1)S(1)}, u32[]{:S(2)}, u32[]{:S(2)}) %all-to-all-start) | async-done | bytes 786464 | tf_op jit(solution)/shard_map/all_to_all | solution.py:477
  90.4 1.4 %shard_map.80 = f32[16,8,256]{2,1,0:T(8,128)} custom-call(bf16[128,24,128]{2,1,0:T(8,128)(2,1)S(1)} %all-to-all-done.got_ref), custom_call_target="tpu_custom_call" | custom-call | tf_op jit(solution)/shard_map/pallas_call | solution.py:312
  91.8 3.5 %all-to-all-start.1 = ((f32[16,8,256]{2,1,0:T(8,128)}), f32[16,8,256]{2,1,0:T(8,128)S(1)}, u32[]{:S(2)}, u32[]{:S(2)}) async-start(f32[16,8,256]{2,1,0:T(8,128)} %shard_map.80), calls=%async_computation.1 | async-start | bytes 262144 | tf_op jit(solution)/shard_map/all_to_all | solution.py:479
  95.7 6.4 %all-to-all-done.1.out_ref = f32[16,8,256]{2,1,0:T(8,128)S(1)} async-done(((f32[16,8,256]{2,1,0:T(8,128)}), f32[16,8,256]{2,1,0:T(8,128)S(1)}, u32[]{:S(2)}, u32[]{:S(2)}) %all-to-all-start.1) | async-done | bytes 131104 | tf_op jit(solution)/shard_map/all_to_all | solution.py:479
  102.1 7.2 %shard_map.81 = f32[8,16,256]{2,1,0:T(8,128)S(1)} custom-call(s32[4]{0:T(128)S(1)} %get-tuple-element.72.flags, f32[16,8,256]{2,1,0:T(8,128)S(1)} %all-to-all-done.1.out_ref, f32[8,4,32,128]{3,2,1,0:T(8,128)S(1)} %get-tuple-element.66.own_hbm, f32[8,4,32,128]{3,2,1,0:T(8,128)S(1)} %collective-permute-done.10.sib_hbm, s32[8,256]{1,0:T(8,128)S(1)} %reshape.46.seq_ref, ...), custom_call_target="tpu_custom_call" | custom-call | tf_op jit(solution)/shard_map/pallas_call | solution.py:382
  109.3 9.5 %all_to_all.15 = f32[8,16,256]{2,1,0:T(8,128)S(1)} all-to-all(f32[8,16,256]{2,1,0:T(8,128)S(1)} %shard_map.81), channel_id=1, replica_groups=mesh['y'=4,'z'=4,'x'=4,'c'=2] {'x','c'}, dimensions={0} | all-to-all | bytes 262144 | tf_op jit(solution)/shard_map/all_to_all | solution.py:481
  (52 shorter events, 8.5 us)
Async XLA Ops:
  0.0 28.1 %collective-permute-start = (bf16[1024,4096]{1,0:T(8,128)(2,1)}, bf16[1024,4096]{1,0:T(8,128)(2,1)}, u32[]{:S(2)}, u32[]{:S(2)}) collective-permute-start(bf16[1024,4096]{1,0:T(8,128)(2,1)} %refs_3_.3), channel_id=1, source_target_pairs={{0,1},{1,0},{2,3},{3,2},{4,5},{5,4},{6,7},{7,6},{8,9},{9,8},{10,11... | collective-permute-start | bytes 25165832 | tf_op jit(solution)/shard_map/ppermute | solution.py:32
  2.5 13.2 %collective-permute-start.1 = (bf16[64,4096]{1,0:T(8,128)(2,1)S(1)}, bf16[64,4096]{1,0:T(8,128)(2,1)S(1)}, u32[]{:S(2)}, u32[]{:S(2)}) collective-permute-start(bf16[64,4096]{1,0:T(8,128)(2,1)S(1)} %constant_dynamic-slice_fusion), channel_id=1, source_target_pairs={{0,2},{1,7},{2,4},{3,1},{4,6},{5,3},{6,0},{7,5},{8,10},{9,15},{10,... | collective-permute-start | bytes 1572872 | tf_op jit(solution)/shard_map/ppermute | solution.py:32
  5.1 11.4 %collective-permute-start.3 = (bf16[64,4096]{1,0:T(8,128)(2,1)S(1)}, bf16[64,4096]{1,0:T(8,128)(2,1)S(1)}, u32[]{:S(2)}, u32[]{:S(2)}) collective-permute-start(bf16[64,4096]{1,0:T(8,128)(2,1)S(1)} %constant_dynamic-slice_fusion), channel_id=1, source_target_pairs={{0,7},{1,2},{2,1},{3,4},{4,3},{5,6},{6,5},{7,0},{8,15},{9,10},{10,... | collective-permute-start | bytes 1572872 | tf_op jit(solution)/shard_map/ppermute | solution.py:32
  5.2 9.5 %collective-permute-start.2 = (bf16[1024,128]{1,0:T(8,128)(2,1)}, bf16[1024,128]{1,0:T(8,128)(2,1)S(1)}, u32[]{:S(2)}, u32[]{:S(2)}) collective-permute-start(bf16[1024,128]{1,0:T(8,128)(2,1)} %own_ref.1), channel_id=1, source_target_pairs={{0,1},{1,0},{2,3},{3,2},{4,5},{5,4},{6,7},{7,6},{8,9},{9,8},{10,11... | collective-permute-start | bytes 786440 | tf_op jit(solution)/shard_map/ppermute | solution.py:32
  17.9 24.5 %collective-permute-start.4 = (bf16[128,4096]{1,0:T(8,128)(2,1)}, bf16[128,4096]{1,0:T(8,128)(2,1)S(1)}, u32[]{:S(2)}, u32[]{:S(2)}) collective-permute-start(bf16[128,4096]{1,0:T(8,128)(2,1)} %get-tuple-element.43), channel_id=1, source_target_pairs={{0,2},{1,7},{2,4},{3,1},{4,6},{5,3},{6,0},{7,5},{8,10},{9,15},{10,... | collective-permute-start | bytes 3145736 | tf_op jit(solution)/shard_map/ppermute | solution.py:32
  21.5 21.0 %collective-permute-start.5 = (bf16[128,4096]{1,0:T(8,128)(2,1)}, bf16[128,4096]{1,0:T(8,128)(2,1)S(1)}, u32[]{:S(2)}, u32[]{:S(2)}) collective-permute-start(bf16[128,4096]{1,0:T(8,128)(2,1)} %get-tuple-element.44.refs_0_), channel_id=1, source_target_pairs={{0,32},{1,97},{2,34},{3,99},{4,36},{5,101},{6,38},{7,103},{8,40},{... | collective-permute-start | bytes 3145736 | tf_op jit(solution)/shard_map/ppermute | solution.py:32
  24.2 18.2 %collective-permute-start.6 = (bf16[128,4096]{1,0:T(8,128)(2,1)}, bf16[128,4096]{1,0:T(8,128)(2,1)S(1)}, u32[]{:S(2)}, u32[]{:S(2)}) collective-permute-start(bf16[128,4096]{1,0:T(8,128)(2,1)} %get-tuple-element.44.refs_0_), channel_id=1, source_target_pairs={{0,8},{1,25},{2,10},{3,27},{4,12},{5,29},{6,14},{7,31},{8,16},{9,1... | collective-permute-start | bytes 3145736 | tf_op jit(solution)/shard_map/ppermute | solution.py:32
  28.1 3.4 %copy-start = (bf16[1024,4096]{1,0:T(8,128)(2,1)S(1)}, bf16[1024,4096]{1,0:T(8,128)(2,1)}, u32[]{:S(2)}) copy-start(bf16[1024,4096]{1,0:T(8,128)(2,1)} %refs_3_.3) | copy-start | bytes 25165828
  31.5 1.6 %copy-start.2 = (bf16[256,4096]{1,0:T(8,128)(2,1)S(1)}, bf16[256,4096]{1,0:T(8,128)(2,1)}, u32[]{:S(2)}) copy-start(bf16[256,4096]{1,0:T(8,128)(2,1)} %refs_0_.1) | copy-start | bytes 6291460
  33.1 1.2 %copy-start.3 = (bf16[4096,128]{1,0:T(8,128)(2,1)S(1)}, bf16[4096,128]{1,0:T(8,128)(2,1)}, u32[]{:S(2)}) copy-start(bf16[4096,128]{1,0:T(8,128)(2,1)} %refs_7_.1) | copy-start | bytes 3145732
  34.3 0.9 copy-start.5
  35.3 9.9 %copy-start.1 = (bf16[1024,4096]{1,0:T(8,128)(2,1)S(1)}, bf16[1024,4096]{1,0:T(8,128)(2,1)}, u32[]{:S(2)}) copy-start(bf16[1024,4096]{1,0:T(8,128)(2,1)} %refs_3_.3) | copy-start | bytes 25165828
  35.3 9.9 %copy-start.4 = (bf16[4096,128]{1,0:T(8,128)(2,1)S(1)}, bf16[4096,128]{1,0:T(8,128)(2,1)}, u32[]{:S(2)}) copy-start(bf16[4096,128]{1,0:T(8,128)(2,1)} %refs_7_.1) | copy-start | bytes 3145732
  35.3 9.9 %copy-start.6 = (bf16[1024,128]{1,0:T(8,128)(2,1)S(1)}, bf16[1024,128]{1,0:T(8,128)(2,1)}, u32[]{:S(2)}) copy-start(bf16[1024,128]{1,0:T(8,128)(2,1)} %own_ref.1) | copy-start | bytes 786436
  42.7 15.8 %collective-permute-start.7 = (bf16[96,4096]{1,0:T(8,128)(2,1)S(1)}, bf16[96,4096]{1,0:T(8,128)(2,1)S(1)}, u32[]{:S(2)}, u32[]{:S(2)}) collective-permute-start(bf16[96,4096]{1,0:T(8,128)(2,1)S(1)} %get-tuple-element.54), channel_id=1, source_target_pairs={{0,32},{1,97},{2,34},{3,99},{4,36},{5,101},{6,38},{7,103},{8,40},{... | collective-permute-start | bytes 2359304 | tf_op jit(solution)/shard_map/ppermute | solution.py:32
  43.2 15.3 %collective-permute-start.8 = (bf16[96,4096]{1,0:T(8,128)(2,1)S(1)}, bf16[96,4096]{1,0:T(8,128)(2,1)S(1)}, u32[]{:S(2)}, u32[]{:S(2)}) collective-permute-start(bf16[96,4096]{1,0:T(8,128)(2,1)S(1)} %get-tuple-element.55), channel_id=1, source_target_pairs={{0,8},{1,25},{2,10},{3,27},{4,12},{5,29},{6,14},{7,31},{8,16},{9,1... | collective-permute-start | bytes 2359304 | tf_op jit(solution)/shard_map/ppermute | solution.py:32
  43.8 14.7 %collective-permute-start.9 = (bf16[64,4096]{1,0:T(8,128)(2,1)S(1)}, bf16[64,4096]{1,0:T(8,128)(2,1)S(1)}, u32[]{:S(2)}, u32[]{:S(2)}) collective-permute-start(bf16[64,4096]{1,0:T(8,128)(2,1)S(1)} %get-tuple-element.56), channel_id=1, source_target_pairs={{0,2},{1,7},{2,4},{3,1},{4,6},{5,3},{6,0},{7,5},{8,10},{9,15},{10,... | collective-permute-start | bytes 1572872 | tf_op jit(solution)/shard_map/ppermute | solution.py:32
  58.5 16.6 %copy-start.7 = (s32[2048]{0:T(1024)S(1)}, s32[2048]{0:T(1024)}, u32[]{:S(2)}) copy-start(s32[2048]{0:T(1024)} %param.12) | copy-start | bytes 24580
  67.5 22.9 %all-to-all-start = ((bf16[128,24,128]{2,1,0:T(8,128)(2,1)}), bf16[128,24,128]{2,1,0:T(8,128)(2,1)S(1)}, u32[]{:S(2)}, u32[]{:S(2)}) async-start(bf16[128,24,128]{2,1,0:T(8,128)(2,1)} %get-tuple-element.65), calls=%async_computation | async-start | bytes 1572864 | tf_op jit(solution)/shard_map/all_to_all | solution.py:477
  73.9 21.8 %collective-permute-start.10 = (f32[8,4,32,128]{3,2,1,0:T(8,128)S(1)}, f32[8,4,32,128]{3,2,1,0:T(8,128)S(1)}, u32[]{:S(2)}, u32[]{:S(2)}) collective-permute-start(f32[8,4,32,128]{3,2,1,0:T(8,128)S(1)} %get-tuple-element.66.own_hbm), channel_id=1, source_target_pairs={{0,1},{1,0},{2,3},{3,2},{4,5},{5,4},{6,7},{7,6},{8,9},{9,8},{10,11... | collective-permute-start | bytes 1572872 | tf_op jit(solution)/shard_map/ppermute | solution.py:32
  91.8 10.3 %all-to-all-start.1 = ((f32[16,8,256]{2,1,0:T(8,128)}), f32[16,8,256]{2,1,0:T(8,128)S(1)}, u32[]{:S(2)}, u32[]{:S(2)}) async-start(f32[16,8,256]{2,1,0:T(8,128)} %shard_map.80), calls=%async_computation.1 | async-start | bytes 262144 | tf_op jit(solution)/shard_map/all_to_all | solution.py:479
